TPU v7x, 256 devices: a whole 4x4x8 slice. The times are simulated.
256 devices in a mesh: strip: 8 (over z), along: 32 (over y, x, core).
Axes of the slice: x: 4, y: 4, z: 8, core: 2. Of those that a mesh axis runs over, the one named last changes fastest.
Arguments:
- heights: float32 [4096, 16384], P('strip', 'along'), may hold values from -6 to 6
- confidence: float32 [4096, 16384], P('strip', 'along'), may hold values from 0.25 to 4
- survey_ids: int32 [4096, 16384], P('strip', 'along'), may hold values from 0 to 39
- seam_mask: int32 [4096, 16384], P('strip', 'along'), may hold values 0 or 1
- datum: float32 [40], replicated, may hold values from -4 to 4
Outputs:
- merged: float32 [4096, 16384], P('strip', 'along')
- offsets: float32 [40, 4096], P(None, 'strip')
All inputs are finite; a program needn't handle non-finite values. No bound on the sum of `seam_mask` on one device may be relied on, other than what follows from the above.
Results may differ from a plain program's by a relative error of at most 0.0003.
Values sent between devices are 32-bit elements; how exact they have to be, the bound alone decides.
A program may use at most 64 MiB of HBM per device.

v0:
```python
import jax
import jax.numpy as jnp
from jax import lax
from jax.sharding import PartitionSpec as P

SURVEYS = 40
SWEEPS = 4


smooth_weight = 1.0
centre_value = 1.05
half_width = 0.95


def with_halo(block, sides, width):
    for axis, dim in sides:
        count = lax.axis_size(axis)
        forward = [(i, i + 1) for i in range(count - 1)]
        backward = [(target, source) for source, target in forward]
        low = lax.ppermute(
            lax.slice_in_dim(block, block.shape[dim] - width, None, axis=dim), axis, forward
        )
        high = lax.ppermute(lax.slice_in_dim(block, 0, width, axis=dim), axis, backward)
        block = jnp.concatenate([low, block, high], axis=dim)
    return block


def neighbour_sum(values):
    padded = with_halo(values, (("strip", 0), ("along", 1)), 1)
    return padded[2:, 1:-1] + padded[:-2, 1:-1] + padded[1:-1, 2:] + padded[1:-1, :-2]


def survey_profile(survey_ids, values):
    row_count, col_count = survey_ids.shape
    block_rows = min(128, row_count)
    block_count = row_count // block_rows
    labels = jnp.arange(SURVEYS, dtype=jnp.int32)[:, None, None]

    def survey_per_block(block):
        ids_block, value_block = block
        matches = ids_block[None] == labels
        return jnp.sum(jnp.where(matches, value_block[None], 0.0), axis=2)

    sums = lax.map(
        survey_per_block,
        (
            survey_ids.reshape(block_count, block_rows, col_count),
            values.reshape(block_count, block_rows, col_count),
        ),
    )
    return sums.transpose(1, 0, 2).reshape(SURVEYS, row_count)


def spread_table(survey_ids, lookup_table):
    row_count, col_count = survey_ids.shape
    block_rows = min(128, row_count)
    block_count = row_count // block_rows
    labels = jnp.arange(SURVEYS, dtype=jnp.int32)[:, None, None]
    blocks = lookup_table.reshape(SURVEYS, block_count, block_rows).transpose(1, 0, 2)

    def spread_per_block(block):
        ids_block, table_block = block
        matches = ids_block[None] == labels
        return jnp.sum(jnp.where(matches, table_block[:, :, None], 0.0), axis=0)

    spread = lax.map(
        spread_per_block, (survey_ids.reshape(block_count, block_rows, col_count), blocks)
    )
    return spread.reshape(row_count, col_count)


def weight_floor(local_profile):
    share_weight = lax.psum(local_profile, "along")
    return jnp.maximum(share_weight, 1.0)


def row_offsets(profile_gap, floor_weight):
    whole_gap = lax.psum(profile_gap, "along")
    return whole_gap / floor_weight


def on_device(heights, confidence, survey_ids, seam_mask, datum):
    row_count = heights.shape[0]
    datum_rows = jnp.broadcast_to(datum[:, None], (SURVEYS, row_count))
    observed = heights + spread_table(survey_ids, datum_rows)
    merged = observed
    diagonal = confidence + 4.0 * smooth_weight
    seam_weight = seam_mask.astype(jnp.float32) * confidence
    local_weight = jnp.sum(seam_weight)
    floor_weight = weight_floor(survey_profile(survey_ids, seam_weight))
    sigma_value = centre_value / half_width
    ratio_now = 1.0 / sigma_value
    direction = jnp.zeros_like(merged)
    offsets = jnp.zeros((SURVEYS, row_count), jnp.float32)
    for sweep_index in range(SWEEPS):
        beside = neighbour_sum(merged)
        gap = seam_weight * (0.25 * beside - observed)
        total_gap, total_weight = lax.psum((jnp.sum(gap), local_weight), ("strip", "along"))
        level = total_gap / (total_weight + 1.0)
        profile_gap = survey_profile(survey_ids, gap)
        offsets = row_offsets(profile_gap, floor_weight) - level
        target = observed + spread_table(survey_ids, offsets)
        residual = confidence * (target - merged) - smooth_weight * (4.0 * merged - beside)
        scaled = residual / diagonal
        if sweep_index == 0:
            direction = scaled / centre_value
        else:
            ratio_next = 1.0 / (2.0 * sigma_value - ratio_now)
            direction = ratio_next * ratio_now * direction + 2.0 * ratio_next / half_width * scaled
            ratio_now = ratio_next
        merged = merged + direction
    return (merged, offsets)


def solution(mesh):
    in_specs = (
        P("strip", "along"),
        P("strip", "along"),
        P("strip", "along"),
        P("strip", "along"),
        P(),
    )
    out_specs = (P("strip", "along"), P(None, "strip"))
    return jax.shard_map(
        on_device, mesh=mesh, in_specs=in_specs, out_specs=out_specs, check_vma=False
    )
```

profile of v0, /device:TPU:1, one launch (start us, length us, event | category | flops | bytes accessed | tf_op | source)
XLA Modules:
  0.0 673.3 jit_solution(18221038500251098762)
XLA Ops:
  8.4 5.2 while.110
  8.4 1.2 select_reduce_fusion.20
  9.7 1.2 select_reduce_fusion.20
  11.0 1.2 select_reduce_fusion.20
  12.3 1.2 select_reduce_fusion.20
  13.6 1.5 bitcast_add_fusion.3
  15.1 1.3 collective-permute-start
  16.4 5.0 collective-permute-start.1
  23.2 5.0 collective-permute-start.2
  28.3 1.9 collective-permute-start.3
  30.2 5.0 while.112
  35.2 3.2 fusion.63
  39.1 11.0 %while.111 = (s32[]{:T(128)}, f32[4,40,128]{2,1,0:T(8,128)}, s32[4,128,512]{2,1,0:T(8,128)S(1)}, f32[4,128,512]{2,1,0:T(8,128)}, s32[]{:T(128)}) while((s32[]{:T(128)}, f32[4,40,128]{2,1,0:T(8,128)}, s32[4,128,512]{2,1,0:T(8,128)S(1)}, f32[4,128,512]{2,1,0:T(8,128)}, s32[]{:T(128)}) %tuple.236), condition=%wide.region_5.6_spmd.clone, body=%wide.region_3.5_spmd.clone.sunk | while | flops 7859202 | bytes 1634885 | solution.py:44
  50.1 1.6 copy_bitcast_fusion.3
  51.7 81.7 %all-reduce = (f32[]{:T(128)}, f32[]{:T(128)}) all-reduce(f32[]{:T(128)} %get-tuple-element.480, f32[]{:T(128)} %get-tuple-element.478), channel_id=1, replica_groups=mesh['strip'=8,'along'=32] {'strip','along'}, use_global_device_ids=true, to_apply=%region_12.13 | all-reduce | flops 2 | bytes 16 | tf_op jit(solution)/shard_map/psum | solution.py:98
  134.9 29.8 %all-reduce.13.cloned.1.call-done = (f32[40,512]{1,0:T(8,128)}, f32[40,512]{1,0:T(8,128)}) async-done(((f32[40,512]{1,0:T(8,128)}, f32[40,512]{1,0:T(8,128)}), (f32[40,512]{1,0:T(8,128)}, f32[40,512]{1,0:T(8,128)})) %all-reduce.13.cloned.1.call-update) | async-done | bytes 163856 | tf_op jit(solution)/shard_map/psum | solution.py:78
  166.7 7.9 %while.113 = (s32[]{:T(128)}, f32[4,128,512]{2,1,0:T(8,128)}, s32[4,128,512]{2,1,0:T(8,128)S(1)}, f32[4,40,128]{2,1,0:T(8,128)S(1)}, s32[]{:T(128)}) while((s32[]{:T(128)}, f32[4,128,512]{2,1,0:T(8,128)}, s32[4,128,512]{2,1,0:T(8,128)S(1)}, f32[4,40,128]{2,1,0:T(8,128)S(1)}, s32[]{:T(128)}) %tuple.228), condition=%wide.region_17.18_spmd.clone, body=%wide.region_15.17_spmd.clone.sunk | while | flops 7798786 | bytes 1634885 | solution.py:66
  166.8 1.2 select_reduce_fusion.23
  168.7 1.2 select_reduce_fusion.23
  170.7 1.2 select_reduce_fusion.23
  172.6 1.2 select_reduce_fusion.23
  174.6 3.5 multiply_add_fusion
  178.1 1.3 collective-permute-start.4
  179.4 4.0 collective-permute-start.5
  185.0 2.8 collective-permute-start.6
  187.8 2.7 collective-permute-start.7
  190.6 2.4 collective-permute-done.6
  192.9 1.3 collective-permute-done.7
  194.2 5.1 fusion.60
  200.0 11.1 %while.114 = (s32[]{:T(128)}, f32[4,40,128]{2,1,0:T(8,128)}, s32[4,128,512]{2,1,0:T(8,128)S(1)}, f32[4,128,512]{2,1,0:T(8,128)}, s32[]{:T(128)}) while((s32[]{:T(128)}, f32[4,40,128]{2,1,0:T(8,128)}, s32[4,128,512]{2,1,0:T(8,128)S(1)}, f32[4,128,512]{2,1,0:T(8,128)}, s32[]{:T(128)}) %tuple.238), condition=%wide.region_20.21_spmd.clone, body=%wide.region_18.20_spmd.clone.sunk | while | flops 7859202 | bytes 1634885 | solution.py:44
  211.0 1.5 copy_bitcast_fusion.2
  212.6 81.3 %psum.84 = f32[]{:T(128)} all-reduce(f32[]{:T(128)} %get-tuple-element.474), channel_id=1, replica_groups=mesh['strip'=8,'along'=32] {'strip','along'}, use_global_device_ids=true, to_apply=%region_23.24 | all-reduce | flops 1 | bytes 8 | tf_op jit(solution)/shard_map/psum | solution.py:98
  294.6 29.7 %all-reduce.7.cloned.1.call-done = f32[40,512]{1,0:T(8,128)} async-done(((f32[40,512]{1,0:T(8,128)}), f32[40,512]{1,0:T(8,128)}) %all-reduce.7.cloned.1.call-update) | async-done | bytes 81936 | tf_op jit(solution)/shard_map/psum | solution.py:78
  324.3 1.5 bitcast_bitcast_fusion.2
  327.0 10.7 %while.115 = (s32[]{:T(128)}, f32[4,128,512]{2,1,0:T(8,128)}, s32[4,128,512]{2,1,0:T(8,128)S(1)}, f32[4,40,128]{2,1,0:T(8,128)}, s32[]{:T(128)}) while((s32[]{:T(128)}, f32[4,128,512]{2,1,0:T(8,128)}, s32[4,128,512]{2,1,0:T(8,128)S(1)}, f32[4,40,128]{2,1,0:T(8,128)}, s32[]{:T(128)}) %tuple.230), condition=%wide.region_26.27_spmd.clone, body=%wide.region_24.26_spmd.clone.sunk | while | flops 7798786 | bytes 1634885 | solution.py:66
  337.7 6.1 fusion.54
  343.9 1.3 collective-permute-start.8
  345.2 4.0 collective-permute-start.9
  350.8 2.6 collective-permute-start.10
  353.4 2.9 collective-permute-start.11
  356.4 2.4 collective-permute-done.10
  358.7 1.3 collective-permute-done.11
  360.0 5.1 fusion.58
  365.8 11.0 %while.116 = (s32[]{:T(128)}, f32[4,40,128]{2,1,0:T(8,128)}, s32[4,128,512]{2,1,0:T(8,128)S(1)}, f32[4,128,512]{2,1,0:T(8,128)}, s32[]{:T(128)}) while((s32[]{:T(128)}, f32[4,40,128]{2,1,0:T(8,128)}, s32[4,128,512]{2,1,0:T(8,128)S(1)}, f32[4,128,512]{2,1,0:T(8,128)}, s32[]{:T(128)}) %tuple.239), condition=%wide.region_29.30_spmd.clone, body=%wide.region_27.29_spmd.clone.sunk | while | flops 7859202 | bytes 1634885 | solution.py:44
  376.8 1.5 copy_bitcast_fusion.1
  378.4 80.8 %psum.86 = f32[]{:T(128)} all-reduce(f32[]{:T(128)} %get-tuple-element.470), channel_id=1, replica_groups=mesh['strip'=8,'along'=32] {'strip','along'}, use_global_device_ids=true, to_apply=%region_32.33 | all-reduce | flops 1 | bytes 8 | tf_op jit(solution)/shard_map/psum | solution.py:98
  459.9 29.9 %all-reduce.9.cloned.1.call-done = f32[40,512]{1,0:T(8,128)} async-done(((f32[40,512]{1,0:T(8,128)}), f32[40,512]{1,0:T(8,128)}) %all-reduce.9.cloned.1.call-update) | async-done | bytes 81936 | tf_op jit(solution)/shard_map/psum | solution.py:78
  489.8 1.5 bitcast_bitcast_fusion.1
  492.4 10.7 %while.117 = (s32[]{:T(128)}, f32[4,128,512]{2,1,0:T(8,128)}, s32[4,128,512]{2,1,0:T(8,128)S(1)}, f32[4,40,128]{2,1,0:T(8,128)}, s32[]{:T(128)}) while((s32[]{:T(128)}, f32[4,128,512]{2,1,0:T(8,128)}, s32[4,128,512]{2,1,0:T(8,128)S(1)}, f32[4,40,128]{2,1,0:T(8,128)}, s32[]{:T(128)}) %tuple.232), condition=%wide.region_35.36_spmd.clone, body=%wide.region_33.35_spmd.clone.sunk | while | flops 7798786 | bytes 1634885 | solution.py:66
  503.2 6.0 fusion.56
  509.2 1.3 collective-permute-start.12
  510.5 4.0 collective-permute-start.13
  516.1 2.6 collective-permute-start.14
  518.7 2.9 collective-permute-start.15
  521.7 2.4 collective-permute-done.14
  524.0 1.3 collective-permute-done.15
  525.3 4.9 fusion.55
  530.2 8.7 %while.118 = (s32[]{:T(128)}, f32[4,40,128]{2,1,0:T(8,128)S(1)}, s32[4,128,512]{2,1,0:T(8,128)S(1)}, f32[4,128,512]{2,1,0:T(8,128)}, s32[]{:T(128)}) while((s32[]{:T(128)}, f32[4,40,128]{2,1,0:T(8,128)S(1)}, s32[4,128,512]{2,1,0:T(8,128)S(1)}, f32[4,128,512]{2,1,0:T(8,128)}, s32[]{:T(128)}) %tuple.237), condition=%wide.region_38.39_spmd.clone, body=%wide.region_36.38_spmd.clone.sunk | while | flops 7859202 | bytes 1634377 | solution.py:44
  539.6 81.1 %psum.88 = f32[]{:T(128)} all-reduce(f32[]{:T(128)} %get-tuple-element.466), channel_id=1, replica_groups=mesh['strip'=8,'along'=32] {'strip','along'}, use_global_device_ids=true, to_apply=%region_41.42 | all-reduce | flops 1 | bytes 8 | tf_op jit(solution)/shard_map/psum | solution.py:98
  621.3 29.7 %all-reduce.11.cloned.1.call-done = f32[40,512]{1,0:T(8,128)} async-done(((f32[40,512]{1,0:T(8,128)}), f32[40,512]{1,0:T(8,128)}) %all-reduce.11.cloned.1.call-update) | async-done | bytes 81936 | tf_op jit(solution)/shard_map/psum | solution.py:78
  653.1 7.9 %while.119 = (s32[]{:T(128)}, f32[4,128,512]{2,1,0:T(8,128)}, s32[4,128,512]{2,1,0:T(8,128)S(1)}, f32[4,40,128]{2,1,0:T(8,128)S(1)}, s32[]{:T(128)}) while((s32[]{:T(128)}, f32[4,128,512]{2,1,0:T(8,128)}, s32[4,128,512]{2,1,0:T(8,128)S(1)}, f32[4,40,128]{2,1,0:T(8,128)S(1)}, s32[]{:T(128)}) %tuple.234), condition=%wide.region_44.45_spmd.clone, body=%wide.region_42.44_spmd.clone.sunk | while | flops 7798786 | bytes 1634885 | solution.py:66
  653.1 1.2 select_reduce_fusion.29
  655.1 1.2 select_reduce_fusion.29
  661.0 5.8 fusion.41
  (210 shorter events, 93.4 us)
Async XLA Ops:
  7.2 1.2 copy-start
  7.2 157.5 %all-reduce.13.cloned.1.call-start = ((), (), s32[]{:S(2)}) async-start(), calls=%async_computation.3 | async-start | bytes 327680 | tf_op jit(solution)/shard_map/psum | solution.py:78
  13.6 7.9 %copy-start.1 = (f32[512,512]{1,0:T(8,128)S(1)}, f32[512,512]{1,0:T(8,128)}, u32[]{:S(2)}) copy-start(f32[512,512]{1,0:T(8,128)} %param.26) | copy-start | bytes 3145732
  13.6 7.9 %copy-start.7 = (s32[512,512]{1,0:T(8,128)S(1)}, s32[512,512]{1,0:T(8,128)}, u32[]{:S(2)}) copy-start(s32[512,512]{1,0:T(8,128)} %param.28) | copy-start | bytes 3145732
  15.1 7.2 %collective-permute-start = (f32[1,512]{1,0:T(1,128)S(1)}, f32[1,512]{1,0:T(1,128)S(1)}, u32[]{:S(2)}, u32[]{:S(2)}) collective-permute-start(f32[1,512]{1,0:T(1,128)S(1)} %get-tuple-element.497), channel_id=1, source_target_pairs={{32,0},{64,32},{96,64},{128,96},{160,128},{192,160},{224,192},{33,... | collective-permute-start | bytes 6152 | tf_op jit(solution)/shard_map/ppermute | solution.py:23
  16.4 6.0 collective-permute-start.1
  23.2 11.9 %collective-permute-start.2 = (f32[514,1]{1,0:T(8,128)}, f32[514,1]{1,0:T(8,128)S(1)}, u32[]{:S(2)}, u32[]{:S(2)}) collective-permute-start(f32[514,1]{1,0:T(8,128)} %get-tuple-element.488), channel_id=1, source_target_pairs={{1,0},{2,1},{3,2},{4,3},{5,4},{6,5},{7,6},{8,7},{9,8},{10,9},{11,1... | collective-permute-start | bytes 6176 | tf_op jit(solution)/shard_map/ppermute | solution.py:23
  28.3 6.9 %collective-permute-start.3 = (f32[514,1]{1,0:T(8,128)}, f32[514,1]{1,0:T(8,128)}, u32[]{:S(2)}, u32[]{:S(2)}) collective-permute-start(f32[514,1]{1,0:T(8,128)} %get-tuple-element.489), channel_id=1, source_target_pairs={{0,1},{1,2},{2,3},{3,4},{4,5},{5,6},{6,7},{7,8},{8,9},{9,10},{10,1... | collective-permute-start | bytes 6176 | tf_op jit(solution)/shard_map/ppermute | solution.py:20
  51.7 272.6 %all-reduce.7.cloned.1.call-start = ((), (), s32[]{:S(2)}) async-start(), calls=%async_computation | async-start | bytes 163840 | tf_op jit(solution)/shard_map/psum | solution.py:78
  178.1 6.0 copy-start.4
  178.1 5.3 collective-permute-start.4
  179.4 4.7 collective-permute-start.5
  185.0 7.9 %collective-permute-start.6 = (f32[514,1]{1,0:T(8,128)}, f32[514,1]{1,0:T(8,128)S(1)}, u32[]{:S(2)}, u32[]{:S(2)}) collective-permute-start(f32[514,1]{1,0:T(8,128)} %get-tuple-element.486), channel_id=1, source_target_pairs={{1,0},{2,1},{3,2},{4,3},{5,4},{6,5},{7,6},{8,7},{9,8},{10,9},{11,1... | collective-permute-start | bytes 6176 | tf_op jit(solution)/shard_map/ppermute | solution.py:23
  187.8 6.4 collective-permute-start.7
  200.0 124.4 %copy-start.6 = (f32[40,512]{1,0:T(8,128)S(1)}, f32[40,512]{1,0:T(8,128)}, u32[]{:S(2)}) copy-start(f32[40,512]{1,0:T(8,128)} %get-tuple-element.465) | copy-start | bytes 245764
  212.6 277.2 %all-reduce.9.cloned.1.call-start = ((), (), s32[]{:S(2)}) async-start(), calls=%async_computation.1 | async-start | bytes 163840 | tf_op jit(solution)/shard_map/psum | solution.py:78
  343.9 6.0 copy-start.3
  343.9 5.3 collective-permute-start.8
  345.2 4.7 collective-permute-start.9
  350.8 7.9 %collective-permute-start.10 = (f32[514,1]{1,0:T(8,128)}, f32[514,1]{1,0:T(8,128)S(1)}, u32[]{:S(2)}, u32[]{:S(2)}) collective-permute-start(f32[514,1]{1,0:T(8,128)} %get-tuple-element.484), channel_id=1, source_target_pairs={{1,0},{2,1},{3,2},{4,3},{5,4},{6,5},{7,6},{8,7},{9,8},{10,9},{11,1... | collective-permute-start | bytes 6176 | tf_op jit(solution)/shard_map/ppermute | solution.py:23
  353.4 6.6 collective-permute-start.11
  378.4 272.6 %all-reduce.11.cloned.1.call-start = ((), (), s32[]{:S(2)}) async-start(), calls=%async_computation.2 | async-start | bytes 163840 | tf_op jit(solution)/shard_map/psum | solution.py:78
  509.2 6.0 copy-start.5
  509.2 5.3 collective-permute-start.12
  510.5 4.7 collective-permute-start.13
  516.1 7.9 %collective-permute-start.14 = (f32[514,1]{1,0:T(8,128)}, f32[514,1]{1,0:T(8,128)S(1)}, u32[]{:S(2)}, u32[]{:S(2)}) collective-permute-start(f32[514,1]{1,0:T(8,128)} %get-tuple-element.482), channel_id=1, source_target_pairs={{1,0},{2,1},{3,2},{4,3},{5,4},{6,5},{7,6},{8,7},{9,8},{10,9},{11,1... | collective-permute-start | bytes 6176 | tf_op jit(solution)/shard_map/ppermute | solution.py:23
  518.7 6.6 collective-permute-start.15
  651.9 1.1 copy-start.8
  653.1 7.9 %copy-start.2 = (f32[512,512]{1,0:T(8,128)S(1)}, f32[512,512]{1,0:T(8,128)}, u32[]{:S(2)}) copy-start(f32[512,512]{1,0:T(8,128)} %param.26) | copy-start | bytes 3145732
Sparse Core Ops, SparseCore 0:
  51.8 112.7 all-reduce.12
  212.7 111.5 all-reduce.6
  378.5 111.2 all-reduce.8
  539.7 111.2 all-reduce.10
where the time goes:
time: 675 us; the launch traced here: 673 us
  blocking collectives  325 us (48%)
  waiting for transfers between devices  132 us (20%)
  other arithmetic  97.2 us (14%)
  local copies, waits for them, and re-layouts  54.7 us (8%)
  starting transfers between devices  45.9 us (7%)
  between operations  17.4 us (3%)
    psum x4, blocking collectives, on_device(): lax.psum((jnp.sum(gap), local_weight), ('strip', 'along'))  325 us
    psum x4, waiting for transfers between devices, row_offsets(): whole_gap = lax.psum(profile_gap, 'along')  119 us
    ppermute x8, starting transfers between devices, with_halo(): lax.ppermute(lax.slice_in_dim(block, block.shape[dim] - width, None, axis...  27.5 us
    reduce_sum x20, other arithmetic, spread_per_block(): return jnp.sum(jnp.where(matches, table_block[:, :, None], 0.0), axis=0)  23.8 us
    reduce_sum x20, other arithmetic, survey_per_block(): return jnp.sum(jnp.where(matches, value_block[None], 0.0), axis=2)  22.7 us
    add x4, other arithmetic, on_device(): merged = merged + direction  21.4 us
    reduce_sum x4, other arithmetic, on_device(): jnp.sum(gap)  18.3 us
    ppermute x8, starting transfers between devices, with_halo(): lax.ppermute(lax.slice_in_dim(block, 0, width, axis=dim), axis, backward)  18.2 us
  transfers between devices with their start and end apart: 20, of which 13 were waited for; matrix products, arithmetic and copies ran while one was open for 1% of the time, Pallas kernels for 0%

commit v1 on v0

v1 whole, which is shorter than its diff:
```python
import functools

import jax
import jax.numpy as jnp
from jax import lax
from jax.experimental import pallas as pl
from jax.experimental.pallas import tpu as pltpu
from jax.sharding import PartitionSpec as P

SURVEYS = 40
SWEEPS = 4

smooth_weight = 1.0
centre_value = 1.05
half_width = 0.95

LANES = 128
DEPTH = 4
MESH = pl.DeviceIdType.MESH
F32 = jnp.float32
BF16 = jnp.bfloat16
I32 = jnp.int32


def coefficients():
    sigma_value = centre_value / half_width
    ratio_now = 1.0 / sigma_value
    pairs = [(0.0, 1.0 / centre_value)]
    for _ in range(SWEEPS - 1):
        ratio_next = 1.0 / (2.0 * sigma_value - ratio_now)
        pairs.append((ratio_next * ratio_now, 2.0 * ratio_next / half_width))
        ratio_now = ratio_next
    return pairs


def torus_distance(step, size):
    return min(step % size, (-step) % size)


def lane_take(values, index):
    return jnp.take_along_axis(values, index, axis=1, mode="promise_in_bounds")


def lanes_of(rows):
    return lax.broadcasted_iota(I32, (rows, LANES), 1)


def kernel(
    zsize,
    dims,
    heights,
    confidence,
    survey_ids,
    seam_mask,
    datum,
    merged_out,
    offsets_out,
    mm,
    ids,
    obs,
    q,
    cq,
    pp,
    w,
    d,
    bes,
    mask,
    onehot,
    dat,
    strip_send,
    strip_recv,
    hist,
    parts,
    floor,
    zsend,
    zrecv,
    table,
    wtotal,
    offs,
    load_sem,
    store_sem,
    strip_ss,
    strip_rs,
    row_ss,
    row_rs,
    part_ss,
    part_rs,
    z_ss,
    z_rs,
    table_ss,
    table_rs,
):
    ny, nx, nc = dims
    along = ny * nx * nc
    rows, cols = heights.shape
    tiles = cols // LANES
    groups = rows // 32
    zi = lax.axis_index("strip")
    me = lax.axis_index("along")
    my_y, my_x, my_c = me // (nx * nc), (me // nc) % nx, me % nc

    steps = [(a, b, c) for a in range(ny) for b in range(nx) for c in range(nc)]
    steps = sorted(steps[1:], key=lambda s: -(torus_distance(s[0], ny) + torus_distance(s[1], nx) + 0.3 * s[2]))

    def partner(step):
        a, b, c = step
        return (((my_y + a) % ny) * nx + (my_x + b) % nx) * nc + (my_c + c) % nc

    def slot_of(step):
        a, b, c = step
        return (((-a) % ny) * nx + (-b) % nx) * nc + (-c) % nc

    loads = []
    for t in range(tiles):
        for n, (src, dst) in enumerate(((survey_ids, ids), (confidence, cq), (heights, obs), (seam_mask, mask))):
            copy = pltpu.make_async_copy(src.at[:, pl.ds(t * LANES, LANES)], dst.at[t], load_sem.at[n, t])
            copy.start()
            loads.append((n, copy))

    mm[:, 0:8, :] = jnp.zeros((tiles + 1, 8, LANES), F32)
    mm[:, rows + 8 : rows + 16, :] = jnp.zeros((tiles + 1, 8, LANES), F32)
    strip_recv[...] = jnp.zeros(strip_recv.shape, F32)

    barrier = pltpu.get_barrier_semaphore()
    for step in steps:
        pl.semaphore_signal(barrier, inc=1, device_id=(zi, partner(step)), device_id_type=MESH)
    for k in range(1, zsize):
        pl.semaphore_signal(barrier, inc=1, device_id=((zi + k) % zsize, me), device_id_type=MESH)

    dat[...] = jnp.zeros((16, LANES), F32)
    dat[:, 0:SURVEYS] = jnp.broadcast_to(datum[...], (16, SURVEYS))

    for n, copy in loads:
        if n < 3:
            copy.wait()

    def pack_strip(b, _):
        r = pl.ds(pl.multiple_of(b * 32, 32), 32)
        lane = lanes_of(32)
        first, last = 0, tiles - 1
        low = jnp.where(lane < 4, ids[first, r, :].astype(F32), pltpu.roll(cq[first, r, :], 4, 1))
        low = jnp.where(lane < 8, low, pltpu.roll(obs[first, r, :], 8, 1))
        high = jnp.where(lane >= 124, ids[last, r, :].astype(F32), pltpu.roll(cq[last, r, :], LANES - 4, 1))
        high = jnp.where(lane >= 120, high, pltpu.roll(obs[last, r, :], LANES - 8, 1))
        bes[0, r, :] = jnp.where(lane < 64, low, high)
        return 0

    lax.fori_loop(0, rows // 32, pack_strip, 0)
    span = min(rows, LANES)
    for b in range(rows // span):
        strip_send[b] = bes[0, b * span : (b + 1) * span, :].T

    pl.semaphore_wait(barrier, along + zsize - 2)

    def strip_copy(side):
        at = pl.ds(0, 16) if side == 0 else pl.ds(112, 16)
        return pltpu.make_async_remote_copy(
            strip_send.at[:, at, :],
            strip_recv.at[:, at, :],
            strip_ss.at[side],
            strip_rs.at[side],
            device_id=(zi, me - 1 if side == 0 else me + 1),
            device_id_type=MESH,
        )

    has = (me > 0, me < along - 1)
    for side in range(2):

        @pl.when(has[side])
        def _():
            strip_copy(side).start()

    def make_onehot(g, _):
        sub = lax.broadcasted_iota(I32, (8, LANES), 0)
        for t in range(tiles):
            block = ids[t, pl.ds(pl.multiple_of(g * 32, 32), 32), :] & 7
            for r in range(0, 32, 2):
                pair = [
                    jnp.where(jnp.broadcast_to(block[r + i : r + i + 1, :], (8, LANES)) == sub, 1.0, 0.0)
                    for i in range(2)
                ]
                onehot[g, r * 8 : r * 8 + 16, t * LANES : (t + 1) * LANES] = jnp.concatenate(pair, 0).astype(BF16)
        return 0

    lax.fori_loop(0, groups, make_onehot, 0)

    def profile(values, hid, g):
        high = values.astype(BF16)
        low = (values - high.astype(F32)).astype(BF16)
        zero = jnp.zeros_like(high)
        match = [hid == h for h in range(5)]
        left = jnp.concatenate([jnp.where(m, p, zero) for p in (high, low) for m in match], 0)
        full = lax.dot_general(left, onehot[g], (((1,), (1,)), ((), ())), preferred_element_type=F32)
        full = full[:160] + full[160:]
        own = lax.broadcasted_iota(I32, (32, 256), 0) == lax.broadcasted_iota(I32, (32, 256), 1) // 8
        sums = [jnp.sum(jnp.where(own, full[32 * h : 32 * h + 32], 0.0), axis=0, keepdims=True) for h in range(5)]
        return jnp.concatenate(sums + [jnp.zeros((3, 256), F32)], 0)

    def high_bits(r):
        return jnp.concatenate([(ids[t, r, :] >> 3) & 7 for t in range(tiles)], 1)

    def put_profile(n, g, sums):
        hist[n, 2 * g] = sums[:, :LANES]
        hist[n, 2 * g + 1] = sums[:, LANES:]

    def part_copy(n, step):
        to = partner(step)
        return pltpu.make_async_remote_copy(
            hist.at[n, to],
            parts.at[n, slot_of(step)],
            part_ss.at[n],
            part_rs.at[n],
            device_id=(zi, to),
            device_id_type=MESH,
        )

    def all_parts(n):
        return pltpu.make_async_remote_copy(
            hist.at[n, pl.ds(1, along - 1)],
            parts.at[n, pl.ds(1, along - 1)],
            part_ss.at[n],
            part_rs.at[n],
            device_id=(zi, me),
            device_id_type=MESH,
        )

    def z_copy(n, k):
        return pltpu.make_async_remote_copy(
            zsend.at[n],
            zrecv.at[n, zsize - k],
            z_ss.at[n],
            z_rs.at[n],
            device_id=((zi + k) % zsize, me),
            device_id_type=MESH,
        )

    def all_z(n):
        return pltpu.make_async_remote_copy(
            zrecv.at[n, pl.ds(1, zsize - 1)],
            zrecv.at[n, pl.ds(1, zsize - 1)],
            z_ss.at[n],
            z_rs.at[n],
            device_id=(zi, me),
            device_id_type=MESH,
        )

    def send_profile(n):
        total = jnp.sum(hist[n], axis=0)
        zsend[n] = total
        zrecv[n, 0] = total
        for k in sorted(range(1, zsize), key=lambda k: -torus_distance(k, zsize)):
            z_copy(n, k).start()
        for step in steps:
            part_copy(n, step).start()
        parts[n, 0] = hist[n, me]

    def summed_parts(n):
        all_parts(n).wait_recv()
        return jnp.sum(parts[n], axis=0)

    def summed_z(n):
        all_z(n).wait_recv()
        return jnp.broadcast_to(jnp.sum(jnp.sum(zrecv[n], axis=0), keepdims=True), (8, LANES))

    for n, copy in loads:
        if n == 3:
            copy.wait()

    def weights(g, _):
        r = pl.ds(pl.multiple_of(g * 32, 32), 32)
        values = []
        for t in range(tiles):
            value = mask[t, r, :].astype(F32) * cq[t, r, :]
            w[t, r, :] = value
            values.append(value)
        put_profile(SWEEPS, g, profile(jnp.concatenate(values, 1), high_bits(r), g))
        return 0

    lax.fori_loop(0, groups, weights, 0)
    send_profile(SWEEPS)

    for side in range(2):

        @pl.when(has[1 - side])
        def _():
            strip_copy(side).wait_recv()

    for b in range(rows // span):
        bes[0, b * span : (b + 1) * span, :] = strip_recv[b].T

    def prepare(b, _):
        r = pl.ds(pl.multiple_of(b * 16, 16), 16)
        lane = lanes_of(16)
        upper = jnp.where(lax.broadcasted_iota(I32, (16, LANES), 0) >= 8, 64, 0)
        got = bes[0, r, :]
        edge_low, edge_high = lane < DEPTH, lane >= LANES - DEPTH
        ids[tiles, r, :] = jnp.where(edge_low | edge_high, got, 0.0).astype(I32)
        cq[tiles, r, :] = jnp.where(
            edge_low, pltpu.roll(got, LANES - 4, 1), jnp.where(edge_high, pltpu.roll(got, 4, 1), 0.0)
        )
        obs[tiles, r, :] = jnp.where(
            edge_low, pltpu.roll(got, LANES - 8, 1), jnp.where(edge_high, pltpu.roll(got, 8, 1), 0.0)
        )
        for t in range(tiles + 1):
            survey = ids[t, r, :]
            weight = cq[t, r, :]
            seen = obs[t, r, :] + lane_take(dat[...], survey)
            inverse = 1.0 / (weight + 4.0 * smooth_weight)
            if t == tiles:
                inside = weight > 0.0
                seen = jnp.where(inside, seen, 0.0)
                inverse = jnp.where(inside, inverse, 0.0)
            share = weight * inverse
            ids[t, r, :] = survey + upper
            obs[t, r, :] = seen
            q[t, r, :] = inverse
            cq[t, r, :] = share
            pp[t, r, :] = share * seen
            mm[t, pl.ds(pl.multiple_of(b * 16 + 8, 8), 16), :] = seen
        return 0

    lax.fori_loop(0, rows // 16, prepare, 0)

    def row_copy(k, side):
        at, to = ((8, rows + 8), (rows + 7, 7))[side]
        return pltpu.make_async_remote_copy(
            mm.at[:, pl.ds(at, 1), :],
            mm.at[:, pl.ds(to, 1), :],
            row_ss.at[k, side],
            row_rs.at[k, side],
            device_id=(zi - 1 if side == 0 else zi + 1, me),
            device_id_type=MESH,
        )

    above = (zi > 0, zi < zsize - 1)

    def send_rows(k):
        for side in range(2):

            @pl.when(above[side])
            def _():
                row_copy(k, side).start()

    def wait_rows(k):
        for side in range(2):

            @pl.when(above[1 - side])
            def _():
                row_copy(k, side).wait_recv()

        for side in range(2):

            @pl.when(above[side])
            def _():
                row_copy(k, side).wait_send()

    send_rows(0)

    def stencil_group(k, g):
        first = g * 32
        r = pl.ds(pl.multiple_of(first, 32), 32)
        lane = lanes_of(32)
        now = [mm[t, pl.ds(pl.multiple_of(first + 8, 8), 32), :] for t in range(tiles + 1)]
        gaps = []
        for t in range(tiles + 1):
            before, after = now[(t - 1) % (tiles + 1)], now[(t + 1) % (tiles + 1)]
            value = mm[t, pl.ds(first + 7, 32), :] + mm[t, pl.ds(first + 9, 32), :]
            value += pltpu.roll(jnp.where(lane == LANES - 1, before, now[t]), 1, 1)
            value += pltpu.roll(jnp.where(lane == 0, after, now[t]), LANES - 1, 1)
            bes[t, r, :] = value
            if t < tiles:
                gaps.append(w[t, r, :] * (0.25 * value - obs[t, r, :]))
        put_profile(k, g, profile(jnp.concatenate(gaps, 1), high_bits(r), g))

    def local_update(k, alpha, beta):
        def block(b, _):
            r = pl.ds(pl.multiple_of(b * 32, 32), 32)
            for t in range(tiles + 1):
                now = mm[t, pl.ds(pl.multiple_of(b * 32 + 8, 8), 32), :]
                value = beta * (pp[t, r, :] + q[t, r, :] * bes[t, r, :] - now)
                if k > 0:
                    value += alpha * d[t, r, :]
                d[t, r, :] = value
            return 0

        lax.fori_loop(0, rows // 32, block, 0)

    def owner_tile(k):
        sums = summed_parts(k)
        if k == 0:
            floor[...] = jnp.maximum(summed_parts(SWEEPS), 1.0)
        share = sums / floor[...]
        lane = lanes_of(8)
        sub = lax.broadcasted_iota(I32, (8, LANES), 0)
        index = 8 * (sub + jnp.where(lane >= 64, 8, 0)) + (lane & 7)
        kind = (lane & 63) >> 3
        tile = jnp.zeros((8, LANES), F32)
        for h in range(5):
            tile = jnp.where(kind == h, lane_take(jnp.broadcast_to(share[h : h + 1], (8, LANES)), index), tile)
        tile = jnp.where(kind == 5, summed_z(k), tile)
        if k == 0:
            tile = jnp.where(kind > 5, summed_z(SWEEPS), tile)
        table[k, me] = tile

    def table_copy(k, step):
        return pltpu.make_async_remote_copy(
            table.at[k, me],
            table.at[k, me],
            table_ss.at[k],
            table_rs.at[k],
            device_id=(zi, partner(step)),
            device_id_type=MESH,
        )

    def all_table(k):
        return pltpu.make_async_remote_copy(
            table.at[k, pl.ds(0, along - 1)],
            table.at[k, pl.ds(0, along - 1)],
            table_ss.at[k],
            table_rs.at[k],
            device_id=(zi, me),
            device_id_type=MESH,
        )

    stores = []
    for k, (alpha, beta) in enumerate(coefficients()):
        last = k == SWEEPS - 1

        def inner(g, _, k=k):
            stencil_group(k, g)
            return 0

        lax.fori_loop(1, groups - 1, inner, 0)
        wait_rows(k)
        stencil_group(k, 0)
        stencil_group(k, groups - 1)
        send_profile(k)
        local_update(k, alpha, beta)

        owner_tile(k)
        for step in steps:
            table_copy(k, step).start()
        all_table(k).wait_recv()

        whole = jnp.sum(table[k], axis=0)
        if k == 0:
            wtotal[...] = lane_take(whole, jnp.full((8, LANES), 48, I32)) + 1.0
        level = lane_take(whole, jnp.full((8, LANES), 40, I32)) / wtotal[...]
        level = jnp.concatenate([level, level], 0)

        def update(b, _, k=k, last=last, beta=beta, level=level):
            r = pl.ds(pl.multiple_of(b * 16, 16), 16)
            at = pl.ds(pl.multiple_of(b * 16 + 8, 8), 16)
            row_table = table[k, b]
            row_table = jnp.concatenate([row_table, row_table], 0) - level
            for t in range(tiles if last else tiles + 1):
                step = d[t, r, :] + beta * cq[t, r, :] * lane_take(row_table, ids[t, r, :])
                if not last:
                    d[t, r, :] = step
                mm[t, at, :] = mm[t, at, :] + step
            return 0

        if not last:
            update(0, 0)
            update(rows // 16 - 1, 0)
            send_rows(k + 1)
            lax.fori_loop(1, rows // 16 - 1, update, 0)
        else:
            chunks = 4
            for c in range(chunks):
                size = rows // chunks
                lax.fori_loop(c * size // 16, (c + 1) * size // 16, update, 0)
                for t in range(tiles):
                    copy = pltpu.make_async_copy(
                        mm.at[t, pl.ds(8 + c * size, size), :],
                        merged_out.at[pl.ds(c * size, size), pl.ds(t * LANES, LANES)],
                        store_sem.at[c, t],
                    )
                    copy.start()
                    stores.append(copy)
            for b in range(rows // span):
                pieces = []
                for o in range(b * span // 16, (b + 1) * span // 16):
                    piece = table[k, o] - level[:8]
                    pieces += [piece, pltpu.roll(piece, 64, 1)]
                offs[:, b * span : (b + 1) * span] = jnp.concatenate(pieces, 0).T[:SURVEYS]
            copy = pltpu.make_async_copy(offs, offsets_out, store_sem.at[chunks, 0])
            copy.start()
            stores.append(copy)

    for side in range(2):

        @pl.when(has[side])
        def _():
            strip_copy(side).wait_send()

    for n in range(SWEEPS + 1):
        all_parts(n).wait_send()
        all_z(n).wait_send()
    for k in range(SWEEPS):
        all_table(k).wait_send()
    for copy in stores:
        copy.wait()


def solution(mesh):
    zsize, along = mesh.shape["strip"], mesh.shape["along"]
    dims = (4, 4, 2) if along == 32 else (1, along // 2, 2)

    def on_device(heights, confidence, survey_ids, seam_mask, datum):
        rows, cols = heights.shape
        assert rows == 16 * along and cols % 256 == 0
        tiles = cols // LANES
        wide = (tiles + 1, rows, LANES)
        narrow = (tiles, rows, LANES)
        span = min(rows, LANES)
        strip = (rows // span, LANES, span)
        dma = pltpu.SemaphoreType.DMA
        scratch = [
            pltpu.VMEM((tiles + 1, rows + 16, LANES), F32),
            pltpu.VMEM(wide, I32),
            pltpu.VMEM(wide, F32),
            pltpu.VMEM(wide, F32),
            pltpu.VMEM(wide, F32),
            pltpu.VMEM(wide, F32),
            pltpu.VMEM(narrow, F32),
            pltpu.VMEM(wide, F32),
            pltpu.VMEM(wide, F32),
            pltpu.VMEM(narrow, I32),
            pltpu.VMEM((rows // 32, 256, cols), BF16),
            pltpu.VMEM((16, LANES), F32),
            pltpu.VMEM(strip, F32),
            pltpu.VMEM(strip, F32),
            pltpu.VMEM((SWEEPS + 1, along, 8, LANES), F32),
            pltpu.VMEM((SWEEPS + 1, along, 8, LANES), F32),
            pltpu.VMEM((8, LANES), F32),
            pltpu.VMEM((SWEEPS + 1, 8, LANES), F32),
            pltpu.VMEM((SWEEPS + 1, zsize, 8, LANES), F32),
            pltpu.VMEM((SWEEPS, along, 8, LANES), F32),
            pltpu.VMEM((8, LANES), F32),
            pltpu.VMEM((SURVEYS, rows), F32),
            dma((4, tiles)),
            dma((5, tiles)),
            dma((2,)),
            dma((2,)),
            dma((SWEEPS, 2)),
            dma((SWEEPS, 2)),
            dma((SWEEPS + 1,)),
            dma((SWEEPS + 1,)),
            dma((SWEEPS + 1,)),
            dma((SWEEPS + 1,)),
            dma((SWEEPS,)),
            dma((SWEEPS,)),
        ]
        return pl.pallas_call(
            functools.partial(kernel, zsize, dims),
            out_shape=(
                jax.ShapeDtypeStruct((rows, cols), F32),
                jax.ShapeDtypeStruct((SURVEYS, rows), F32),
            ),
            in_specs=[pl.BlockSpec(memory_space=pl.ANY)] * 4 + [pl.BlockSpec(memory_space=pltpu.VMEM)],
            out_specs=(pl.BlockSpec(memory_space=pl.ANY), pl.BlockSpec(memory_space=pl.ANY)),
            scratch_shapes=scratch,
            compiler_params=pltpu.CompilerParams(
                collective_id=0, has_side_effects=True, vmem_limit_bytes=44 * 1024 * 1024
            ),
        )(heights, confidence, survey_ids, seam_mask, datum.reshape(1, SURVEYS))

    return jax.shard_map(
        on_device,
        mesh=mesh,
        in_specs=(P("strip", "along"),) * 4 + (P(),),
        out_specs=(P("strip", "along"), P(None, "strip")),
        check_vma=False,
    )
```

time: 675 us -> 102 us (0.15)
  blocking collectives: 325 us -> 0 us
  waiting for transfers between devices: 132 us -> 0 us
  other arithmetic: 97.2 us -> 0 us
  Pallas kernels: 0 us -> 93.9 us
  local copies, waits for them, and re-layouts: 54.7 us -> 7.15 us
  starting transfers between devices: 45.9 us -> 0 us
  between operations: 17.4 us -> 0.65 us
    psum x4 -> x0, blocking collectives: 325 us -> none  [on_device(): lax.psum((jnp.sum(gap), local_weight), ('strip', 'along'))]
    psum x4 -> x0, waiting for transfers between devices: 119 us -> none  [row_offsets(): whole_gap = lax.psum(profile_gap, 'along')]
    pallas_call x0 -> x1, Pallas kernels: none -> 93.9 us  [on_device(): pl.pallas_call(functools.partial(kernel, zsize, dims), out_shape=(jax.Sha...]
    reduce_sum x45 -> x0, other arithmetic: 65.7 us -> none  [the longest x20 23.8 us: spread_per_block(): return jnp.sum(jnp.where(matches, table_block[:, :, None], 0.0), axis=0)]
    ppermute x16 -> x0, starting transfers between devices: 45.7 us -> none  [the longest x8 27.5 us: with_halo(): lax.ppermute(lax.slice_in_dim(block, block.shape[dim] - width, None, axis...]
    add x5 -> x0, other arithmetic: 22.9 us -> none  [the longest x4 21.4 us: on_device(): merged = merged + direction]
    broadcast_in_dim x40 -> x0, local copies, waits for them, and re-layouts: 21.6 us -> none  [the longest x20 15.6 us: survey_per_block(): return jnp.sum(jnp.where(matches, value_block[None], 0.0), axis=2)]
    dynamic_update_slice x40 -> x0, local copies, waits for them, and re-layouts: 19.3 us -> none  [the longest x20 11.8 us: spread_table(): lax.map(spread_per_block, (survey_ids.reshape(block_count, block_rows, co...]
  transfers between devices with their start and end apart: 20 -> 0, of which waited for: 13 -> 0; matrix products, arithmetic and copies ran while one was open for 1% -> 0% of each run, Pallas kernels for 0% -> 0%
where the time goes in v1:
time: 102 us
  Pallas kernels  93.9 us (92%)
  local copies, waits for them, and re-layouts  7.15 us (7%)
    pallas_call x1, Pallas kernels, on_device(): pl.pallas_call(functools.partial(kernel, zsize, dims), out_shape=(jax.Sha...  93.9 us
    unnamed x12, local copies, waits for them, and re-layouts  7.15 us

profile of v1, /device:TPU:1, one launch (start us, length us, event | category | flops | bytes accessed | tf_op | source)
XLA Modules:
  0.0 101.7 jit_solution(6448640460442889774)
XLA Ops:
  0.6 0.0 copy-start.4
  0.6 0.6 copy-done.4
  1.3 0.0 copy-start
  1.3 1.2 %copy-done = f32[512,512]{1,0:T(8,128)S(1)} copy-done((f32[512,512]{1,0:T(8,128)S(1)}, f32[512,512]{1,0:T(8,128)}, u32[]{:S(2)}) %copy-start) | copy-done | bytes 1048600
  2.5 0.0 copy-start.1
  2.5 1.2 %copy-done.1 = f32[512,512]{1,0:T(8,128)S(1)} copy-done((f32[512,512]{1,0:T(8,128)S(1)}, f32[512,512]{1,0:T(8,128)}, u32[]{:S(2)}) %copy-start.1) | copy-done | bytes 1048600
  3.7 0.0 copy-start.2
  3.7 1.2 %copy-done.2 = s32[512,512]{1,0:T(8,128)S(1)} copy-done((s32[512,512]{1,0:T(8,128)S(1)}, s32[512,512]{1,0:T(8,128)}, u32[]{:S(2)}) %copy-start.2) | copy-done | bytes 1048600
  5.0 0.0 copy-start.3
  5.0 1.2 %copy-done.3 = s32[512,512]{1,0:T(8,128)S(1)} copy-done((s32[512,512]{1,0:T(8,128)S(1)}, s32[512,512]{1,0:T(8,128)}, u32[]{:S(2)}) %copy-start.3) | copy-done | bytes 1048600
  6.2 93.9 %shard_map.68 = (f32[512,512]{1,0:T(8,128)S(1)}, f32[40,512]{1,0:T(8,128)S(1)}) custom-call(f32[512,512]{1,0:T(8,128)S(1)} %copy-done, f32[512,512]{1,0:T(8,128)S(1)} %copy-done.1, s32[512,512]{1,0:T(8,128)S(1)} %copy-done.2, s32[512,512]{1,0:T(8,128)S(1)} %copy-done.3, f32[1,40]{1,0:T(1,128)S(1)} %bitcast.1), custom_call_target="tpu_custom_call" | custom-call | tf_op jit(solution)/shard_map/pallas_call | solution.py:555
  100.1 1.0 copy.9
  101.1 0.6 copy.10
Async XLA Ops:
  0.6 0.7 copy-start.4
  1.3 1.2 %copy-start = (f32[512,512]{1,0:T(8,128)S(1)}, f32[512,512]{1,0:T(8,128)}, u32[]{:S(2)}) copy-start(f32[512,512]{1,0:T(8,128)} %heights.1) | copy-start | bytes 3145732
  2.5 1.2 %copy-start.1 = (f32[512,512]{1,0:T(8,128)S(1)}, f32[512,512]{1,0:T(8,128)}, u32[]{:S(2)}) copy-start(f32[512,512]{1,0:T(8,128)} %confidence.1) | copy-start | bytes 3145732
  3.7 1.2 %copy-start.2 = (s32[512,512]{1,0:T(8,128)S(1)}, s32[512,512]{1,0:T(8,128)}, u32[]{:S(2)}) copy-start(s32[512,512]{1,0:T(8,128)} %survey_ids.1) | copy-start | bytes 3145732
  5.0 1.2 %copy-start.3 = (s32[512,512]{1,0:T(8,128)S(1)}, s32[512,512]{1,0:T(8,128)}, u32[]{:S(2)}) copy-start(s32[512,512]{1,0:T(8,128)} %seam_mask.1) | copy-start | bytes 3145732

commit v2 on v1

--- a/solution.py
+++ b/solution.py
@@ -145,7 +145,7 @@
         bes[0, r, :] = jnp.where(lane < 64, low, high)
         return 0
 
-    lax.fori_loop(0, rows // 32, pack_strip, 0)
+    lax.fori_loop(0, rows // 32, pack_strip, 0, unroll=4)
     span = min(rows, LANES)
     for b in range(rows // span):
         strip_send[b] = bes[0, b * span : (b + 1) * span, :].T
@@ -182,7 +182,7 @@
                 onehot[g, r * 8 : r * 8 + 16, t * LANES : (t + 1) * LANES] = jnp.concatenate(pair, 0).astype(BF16)
         return 0
 
-    lax.fori_loop(0, groups, make_onehot, 0)
+    lax.fori_loop(0, groups, make_onehot, 0, unroll=4)
 
     def profile(values, hid, g):
         high = values.astype(BF16)
@@ -276,7 +276,7 @@
         put_profile(SWEEPS, g, profile(jnp.concatenate(values, 1), high_bits(r), g))
         return 0
 
-    lax.fori_loop(0, groups, weights, 0)
+    lax.fori_loop(0, groups, weights, 0, unroll=8)
     send_profile(SWEEPS)
 
     for side in range(2):
@@ -319,7 +319,7 @@
             mm[t, pl.ds(pl.multiple_of(b * 16 + 8, 8), 16), :] = seen
         return 0
 
-    lax.fori_loop(0, rows // 16, prepare, 0)
+    lax.fori_loop(0, rows // 16, prepare, 0, unroll=4)
 
     def row_copy(k, side):
         at, to = ((8, rows + 8), (rows + 7, 7))[side]
@@ -383,7 +383,7 @@
                 d[t, r, :] = value
             return 0
 
-        lax.fori_loop(0, rows // 32, block, 0)
+        lax.fori_loop(0, rows // 32, block, 0, unroll=4)
 
     def owner_tile(k):
         sums = summed_parts(k)
@@ -430,7 +430,7 @@
             stencil_group(k, g)
             return 0
 
-        lax.fori_loop(1, groups - 1, inner, 0)
+        lax.fori_loop(1, groups - 1, inner, 0, unroll=7)
         wait_rows(k)
         stencil_group(k, 0)
         stencil_group(k, groups - 1)
@@ -464,12 +464,12 @@
             update(0, 0)
             update(rows // 16 - 1, 0)
             send_rows(k + 1)
-            lax.fori_loop(1, rows // 16 - 1, update, 0)
+            lax.fori_loop(1, rows // 16 - 1, update, 0, unroll=5)
         else:
             chunks = 4
             for c in range(chunks):
                 size = rows // chunks
-                lax.fori_loop(c * size // 16, (c + 1) * size // 16, update, 0)
+                lax.fori_loop(c * size // 16, (c + 1) * size // 16, update, 0, unroll=4)
                 for t in range(tiles):
                     copy = pltpu.make_async_copy(
                         mm.at[t, pl.ds(8 + c * size, size), :],
@@ -562,7 +562,7 @@
             out_specs=(pl.BlockSpec(memory_space=pl.ANY), pl.BlockSpec(memory_space=pl.ANY)),
             scratch_shapes=scratch,
             compiler_params=pltpu.CompilerParams(
-                collective_id=0, has_side_effects=True, vmem_limit_bytes=44 * 1024 * 1024
+                collective_id=0, has_side_effects=True, vmem_limit_bytes=60 * 1024 * 1024
             ),
         )(heights, confidence, survey_ids, seam_mask, datum.reshape(1, SURVEYS))
 

time: 102 us -> 78.1 us (0.77)
  Pallas kernels: 93.9 us -> 74.4 us
  local copies, waits for them, and re-layouts: 7.15 us -> 2.93 us
    pallas_call x1, Pallas kernels: 93.9 us -> 74.4 us  [on_device(): pl.pallas_call(functools.partial(kernel, zsize, dims), out_shape=(jax.Sha...]
    unnamed x12 -> x4, local copies, waits for them, and re-layouts: 7.15 us -> 2.93 us
where the time goes in v2:
time: 78.1 us; the launch traced here: 78 us
  Pallas kernels  74.4 us (95%)
  local copies, waits for them, and re-layouts  2.93 us (4%)
    pallas_call x1, Pallas kernels, on_device(): pl.pallas_call(functools.partial(kernel, zsize, dims), out_shape=(jax.Sha...  74.4 us
    unnamed x4, local copies, waits for them, and re-layouts  2.93 us

profile of v2, /device:TPU:1, one launch (start us, length us, event | category | flops | bytes accessed | tf_op | source)
XLA Modules:
  0.0 78.0 jit_solution(12201187650964818610)
XLA Ops:
  0.6 74.4 %shard_map.68 = (f32[512,512]{1,0:T(8,128)}, f32[40,512]{1,0:T(8,128)}) custom-call(f32[512,512]{1,0:T(8,128)} %heights.1, f32[512,512]{1,0:T(8,128)} %confidence.1, s32[512,512]{1,0:T(8,128)} %survey_ids.1, s32[512,512]{1,0:T(8,128)} %seam_mask.1, f32[1,40]{1,0:T(1,128)} %bitcast.1), custom_call_target="tpu_custom_call" | custom-call | tf_op jit(solution)/shard_map/pallas_call | solution.py:555
  75.0 0.0 copy-start
  75.0 2.3 %copy.9 = f32[512,512]{1,0:T(8,128)} copy(f32[512,512]{1,0:T(8,128)} %get-tuple-element.4) | data formatting | bytes 2097152
  77.3 0.0 copy-done
  77.3 0.6 copy.10
Async XLA Ops:
  75.0 2.3 %copy-start = (f32[40,512]{1,0:T(8,128)S(1)}, f32[40,512]{1,0:T(8,128)}, u32[]{:S(2)}) copy-start(f32[40,512]{1,0:T(8,128)} %get-tuple-element.5) | copy-start | bytes 245764

commit v3 on v2

--- a/solution.py
+++ b/solution.py
@@ -66,6 +66,7 @@
     bes,
     mask,
     onehot,
+    datum_row,
     dat,
     strip_send,
     strip_recv,
@@ -117,6 +118,9 @@
             copy.start()
             loads.append((n, copy))
 
+    datum_copy = pltpu.make_async_copy(datum, datum_row, load_sem.at[4, 0])
+    datum_copy.start()
+
     mm[:, 0:8, :] = jnp.zeros((tiles + 1, 8, LANES), F32)
     mm[:, rows + 8 : rows + 16, :] = jnp.zeros((tiles + 1, 8, LANES), F32)
     strip_recv[...] = jnp.zeros(strip_recv.shape, F32)
@@ -127,12 +131,12 @@
     for k in range(1, zsize):
         pl.semaphore_signal(barrier, inc=1, device_id=((zi + k) % zsize, me), device_id_type=MESH)
 
-    dat[...] = jnp.zeros((16, LANES), F32)
-    dat[:, 0:SURVEYS] = jnp.broadcast_to(datum[...], (16, SURVEYS))
-
     for n, copy in loads:
         if n < 3:
             copy.wait()
+    datum_copy.wait()
+    dat[...] = jnp.zeros((16, LANES), F32)
+    dat[:, 0:SURVEYS] = jnp.broadcast_to(datum_row[...], (16, SURVEYS))
 
     def pack_strip(b, _):
         r = pl.ds(pl.multiple_of(b * 32, 32), 32)
@@ -170,7 +174,7 @@
         def _():
             strip_copy(side).start()
 
-    def make_onehot(g, _):
+    def make_onehot(g):
         sub = lax.broadcasted_iota(I32, (8, LANES), 0)
         for t in range(tiles):
             block = ids[t, pl.ds(pl.multiple_of(g * 32, 32), 32), :] & 7
@@ -180,9 +184,6 @@
                     for i in range(2)
                 ]
                 onehot[g, r * 8 : r * 8 + 16, t * LANES : (t + 1) * LANES] = jnp.concatenate(pair, 0).astype(BF16)
-        return 0
-
-    lax.fori_loop(0, groups, make_onehot, 0, unroll=4)
 
     def profile(values, hid, g):
         high = values.astype(BF16)
@@ -191,17 +192,29 @@
         match = [hid == h for h in range(5)]
         left = jnp.concatenate([jnp.where(m, p, zero) for p in (high, low) for m in match], 0)
         full = lax.dot_general(left, onehot[g], (((1,), (1,)), ((), ())), preferred_element_type=F32)
-        full = full[:160] + full[160:]
-        own = lax.broadcasted_iota(I32, (32, 256), 0) == lax.broadcasted_iota(I32, (32, 256), 1) // 8
-        sums = [jnp.sum(jnp.where(own, full[32 * h : 32 * h + 32], 0.0), axis=0, keepdims=True) for h in range(5)]
-        return jnp.concatenate(sums + [jnp.zeros((3, 256), F32)], 0)
+        lane = lanes_of(8)
+        sub = lax.broadcasted_iota(I32, (8, LANES), 0)
+        own_row = (lane >> 3) & 7
+        out = []
+        for j in range(2):
+            tile = jnp.zeros((8, LANES), F32)
+            for h in range(5):
+                value = 0.0
+                for part in range(2):
+                    at = (part * 5 + h) * 32 + 16 * j
+                    pair = [full[at + 8 * i : at + 8 * i + 8, j * LANES : (j + 1) * LANES] for i in range(2)]
+                    value += jnp.where(lane < 64, pair[0], pair[1])
+                value = jnp.take_along_axis(value, own_row, axis=0, mode="promise_in_bounds")
+                tile = jnp.where(sub == h, value, tile)
+            out.append(tile)
+        return out
 
     def high_bits(r):
         return jnp.concatenate([(ids[t, r, :] >> 3) & 7 for t in range(tiles)], 1)
 
     def put_profile(n, g, sums):
-        hist[n, 2 * g] = sums[:, :LANES]
-        hist[n, 2 * g + 1] = sums[:, LANES:]
+        hist[n, 2 * g] = sums[0]
+        hist[n, 2 * g + 1] = sums[1]
 
     def part_copy(n, step):
         to = partner(step)
@@ -266,17 +279,74 @@
         if n == 3:
             copy.wait()
 
-    def weights(g, _):
+    def row_copy(k, n, side):
+        at, to = ((8, rows + 8), (rows + 7, 7))[side]
+        which = pl.ds(0, tiles) if n == SWEEPS else pl.ds(tiles, 1) if k == 0 else pl.ds(0, tiles + 1)
+        return pltpu.make_async_remote_copy(
+            mm.at[which, pl.ds(at, 1), :],
+            mm.at[which, pl.ds(to, 1), :],
+            row_ss.at[n, side],
+            row_rs.at[n, side],
+            device_id=(zi - 1 if side == 0 else zi + 1, me),
+            device_id_type=MESH,
+        )
+
+    above = (zi > 0, zi < zsize - 1)
+
+    def send_rows(k, n):
+        for side in range(2):
+
+            @pl.when(above[side])
+            def _():
+                row_copy(k, n, side).start()
+
+    def wait_rows(k, n):
+        for side in range(2):
+
+            @pl.when(above[1 - side])
+            def _():
+                row_copy(k, n, side).wait_recv()
+
+        for side in range(2):
+
+            @pl.when(above[side])
+            def _():
+                row_copy(k, n, side).wait_send()
+
+    def prepare(g, t):
         r = pl.ds(pl.multiple_of(g * 32, 32), 32)
+        upper = jnp.where(lax.broadcasted_iota(I32, (32, LANES), 0) & 8 > 0, 64, 0)
+        survey = ids[t, r, :]
+        weight = cq[t, r, :]
+        seen = obs[t, r, :] + lane_take(jnp.concatenate([dat[...]] * 2, 0), survey)
+        inverse = 1.0 / (weight + 4.0 * smooth_weight)
+        if t == tiles:
+            inside = weight > 0.0
+            seen = jnp.where(inside, seen, 0.0)
+            inverse = jnp.where(inside, inverse, 0.0)
+        share = weight * inverse
+        ids[t, r, :] = survey + upper
+        obs[t, r, :] = seen
+        q[t, r, :] = inverse
+        cq[t, r, :] = share
+        pp[t, r, :] = share * seen
+        mm[t, pl.ds(pl.multiple_of(g * 32 + 8, 8), 32), :] = seen
+
+    def start_group(g, _):
+        r = pl.ds(pl.multiple_of(g * 32, 32), 32)
+        make_onehot(g)
         values = []
         for t in range(tiles):
             value = mask[t, r, :].astype(F32) * cq[t, r, :]
             w[t, r, :] = value
             values.append(value)
         put_profile(SWEEPS, g, profile(jnp.concatenate(values, 1), high_bits(r), g))
+        for t in range(tiles):
+            prepare(g, t)
         return 0
 
-    lax.fori_loop(0, groups, weights, 0, unroll=8)
+    lax.fori_loop(0, groups, start_group, 0, unroll=4)
+    send_rows(0, SWEEPS)
     send_profile(SWEEPS)
 
     for side in range(2):
@@ -288,10 +358,9 @@
     for b in range(rows // span):
         bes[0, b * span : (b + 1) * span, :] = strip_recv[b].T
 
-    def prepare(b, _):
-        r = pl.ds(pl.multiple_of(b * 16, 16), 16)
-        lane = lanes_of(16)
-        upper = jnp.where(lax.broadcasted_iota(I32, (16, LANES), 0) >= 8, 64, 0)
+    def unpack_strip(g, _):
+        r = pl.ds(pl.multiple_of(g * 32, 32), 32)
+        lane = lanes_of(32)
         got = bes[0, r, :]
         edge_low, edge_high = lane < DEPTH, lane >= LANES - DEPTH
         ids[tiles, r, :] = jnp.where(edge_low | edge_high, got, 0.0).astype(I32)
@@ -301,60 +370,11 @@
         obs[tiles, r, :] = jnp.where(
             edge_low, pltpu.roll(got, LANES - 8, 1), jnp.where(edge_high, pltpu.roll(got, 8, 1), 0.0)
         )
-        for t in range(tiles + 1):
-            survey = ids[t, r, :]
-            weight = cq[t, r, :]
-            seen = obs[t, r, :] + lane_take(dat[...], survey)
-            inverse = 1.0 / (weight + 4.0 * smooth_weight)
-            if t == tiles:
-                inside = weight > 0.0
-                seen = jnp.where(inside, seen, 0.0)
-                inverse = jnp.where(inside, inverse, 0.0)
-            share = weight * inverse
-            ids[t, r, :] = survey + upper
-            obs[t, r, :] = seen
-            q[t, r, :] = inverse
-            cq[t, r, :] = share
-            pp[t, r, :] = share * seen
-            mm[t, pl.ds(pl.multiple_of(b * 16 + 8, 8), 16), :] = seen
+        prepare(g, tiles)
         return 0
 
-    lax.fori_loop(0, rows // 16, prepare, 0, unroll=4)
-
-    def row_copy(k, side):
-        at, to = ((8, rows + 8), (rows + 7, 7))[side]
-        return pltpu.make_async_remote_copy(
-            mm.at[:, pl.ds(at, 1), :],
-            mm.at[:, pl.ds(to, 1), :],
-            row_ss.at[k, side],
-            row_rs.at[k, side],
-            device_id=(zi - 1 if side == 0 else zi + 1, me),
-            device_id_type=MESH,
-        )
-
-    above = (zi > 0, zi < zsize - 1)
-
-    def send_rows(k):
-        for side in range(2):
-
-            @pl.when(above[side])
-            def _():
-                row_copy(k, side).start()
-
-    def wait_rows(k):
-        for side in range(2):
-
-            @pl.when(above[1 - side])
-            def _():
-                row_copy(k, side).wait_recv()
-
-        for side in range(2):
-
-            @pl.when(above[side])
-            def _():
-                row_copy(k, side).wait_send()
-
-    send_rows(0)
+    lax.fori_loop(0, groups, unpack_strip, 0, unroll=4)
+    send_rows(0, 0)
 
     def stencil_group(k, g):
         first = g * 32
@@ -386,10 +406,11 @@
         lax.fori_loop(0, rows // 32, block, 0, unroll=4)
 
     def owner_tile(k):
-        sums = summed_parts(k)
+        gap_total = summed_z(k)
         if k == 0:
-            floor[...] = jnp.maximum(summed_parts(SWEEPS), 1.0)
-        share = sums / floor[...]
+            weight_total = summed_z(SWEEPS)
+            floor[...] = 1.0 / jnp.maximum(summed_parts(SWEEPS), 1.0)
+        share = summed_parts(k) * floor[...]
         lane = lanes_of(8)
         sub = lax.broadcasted_iota(I32, (8, LANES), 0)
         index = 8 * (sub + jnp.where(lane >= 64, 8, 0)) + (lane & 7)
@@ -397,9 +418,9 @@
         tile = jnp.zeros((8, LANES), F32)
         for h in range(5):
             tile = jnp.where(kind == h, lane_take(jnp.broadcast_to(share[h : h + 1], (8, LANES)), index), tile)
-        tile = jnp.where(kind == 5, summed_z(k), tile)
+        tile = jnp.where(kind == 5, gap_total, tile)
         if k == 0:
-            tile = jnp.where(kind > 5, summed_z(SWEEPS), tile)
+            tile = jnp.where(kind > 5, weight_total, tile)
         table[k, me] = tile
 
     def table_copy(k, step):
@@ -422,16 +443,43 @@
             device_id_type=MESH,
         )
 
+    def update_group(g, beta, level, last):
+        r = pl.ds(pl.multiple_of(g * 32, 32), 32)
+        at = pl.ds(pl.multiple_of(g * 32 + 8, 8), 32)
+        row_table = [table[last, 2 * g + i] for i in (0, 0, 1, 1)]
+        row_table = jnp.concatenate(row_table, 0) - level
+        for t in range(tiles if last == SWEEPS - 1 else tiles + 1):
+            step = d[t, r, :] + beta * cq[t, r, :] * lane_take(row_table, ids[t, r, :])
+            if last < SWEEPS - 1:
+                d[t, r, :] = step
+            mm[t, at, :] = mm[t, at, :] + step
+
     stores = []
+    level, before = None, None
     for k, (alpha, beta) in enumerate(coefficients()):
-        last = k == SWEEPS - 1
-
-        def inner(g, _, k=k):
-            stencil_group(k, g)
-            return 0
-
-        lax.fori_loop(1, groups - 1, inner, 0, unroll=7)
-        wait_rows(k)
+        if k == 0:
+
+            def first(g, _):
+                stencil_group(0, g)
+                return 0
+
+            lax.fori_loop(1, groups - 1, first, 0, unroll=14)
+            wait_rows(0, SWEEPS)
+            wait_rows(0, 0)
+        else:
+            update_group(0, before, level, k - 1)
+            update_group(groups - 1, before, level, k - 1)
+            send_rows(k, k)
+            update_group(1, before, level, k - 1)
+
+            def both(g, _, k=k, before=before, level=level):
+                update_group(g + 1, before, level, k - 1)
+                stencil_group(k, g)
+                return 0
+
+            lax.fori_loop(1, groups - 2, both, 0, unroll=13)
+            stencil_group(k, groups - 2)
+            wait_rows(k, k)
         stencil_group(k, 0)
         stencil_group(k, groups - 1)
         send_profile(k)
@@ -446,47 +494,35 @@
         if k == 0:
             wtotal[...] = lane_take(whole, jnp.full((8, LANES), 48, I32)) + 1.0
         level = lane_take(whole, jnp.full((8, LANES), 40, I32)) / wtotal[...]
-        level = jnp.concatenate([level, level], 0)
-
-        def update(b, _, k=k, last=last, beta=beta, level=level):
-            r = pl.ds(pl.multiple_of(b * 16, 16), 16)
-            at = pl.ds(pl.multiple_of(b * 16 + 8, 8), 16)
-            row_table = table[k, b]
-            row_table = jnp.concatenate([row_table, row_table], 0) - level
-            for t in range(tiles if last else tiles + 1):
-                step = d[t, r, :] + beta * cq[t, r, :] * lane_take(row_table, ids[t, r, :])
-                if not last:
-                    d[t, r, :] = step
-                mm[t, at, :] = mm[t, at, :] + step
+        level = jnp.concatenate([level] * 4, 0)
+        before = beta
+
+    chunks = 4
+    for c in range(chunks):
+        size = rows // chunks
+
+        def final(g, _, level=level):
+            update_group(g, before, level, SWEEPS - 1)
             return 0
 
-        if not last:
-            update(0, 0)
-            update(rows // 16 - 1, 0)
-            send_rows(k + 1)
-            lax.fori_loop(1, rows // 16 - 1, update, 0, unroll=5)
-        else:
-            chunks = 4
-            for c in range(chunks):
-                size = rows // chunks
-                lax.fori_loop(c * size // 16, (c + 1) * size // 16, update, 0, unroll=4)
-                for t in range(tiles):
-                    copy = pltpu.make_async_copy(
-                        mm.at[t, pl.ds(8 + c * size, size), :],
-                        merged_out.at[pl.ds(c * size, size), pl.ds(t * LANES, LANES)],
-                        store_sem.at[c, t],
-                    )
-                    copy.start()
-                    stores.append(copy)
-            for b in range(rows // span):
-                pieces = []
-                for o in range(b * span // 16, (b + 1) * span // 16):
-                    piece = table[k, o] - level[:8]
-                    pieces += [piece, pltpu.roll(piece, 64, 1)]
-                offs[:, b * span : (b + 1) * span] = jnp.concatenate(pieces, 0).T[:SURVEYS]
-            copy = pltpu.make_async_copy(offs, offsets_out, store_sem.at[chunks, 0])
+        lax.fori_loop(c * size // 32, (c + 1) * size // 32, final, 0, unroll=4)
+        for t in range(tiles):
+            copy = pltpu.make_async_copy(
+                mm.at[t, pl.ds(8 + c * size, size), :],
+                merged_out.at[pl.ds(c * size, size), pl.ds(t * LANES, LANES)],
+                store_sem.at[c, t],
+            )
             copy.start()
             stores.append(copy)
+    for b in range(rows // span):
+        pieces = []
+        for o in range(b * span // 16, (b + 1) * span // 16):
+            piece = table[SWEEPS - 1, o] - level[:8]
+            pieces += [piece, pltpu.roll(piece, 64, 1)]
+        offs[:, b * span : (b + 1) * span] = jnp.concatenate(pieces, 0).T[:SURVEYS]
+    copy = pltpu.make_async_copy(offs, offsets_out, store_sem.at[chunks, 0])
+    copy.start()
+    stores.append(copy)
 
     for side in range(2):
 
@@ -528,6 +564,7 @@
             pltpu.VMEM(wide, F32),
             pltpu.VMEM(narrow, I32),
             pltpu.VMEM((rows // 32, 256, cols), BF16),
+            pltpu.VMEM((1, SURVEYS), F32),
             pltpu.VMEM((16, LANES), F32),
             pltpu.VMEM(strip, F32),
             pltpu.VMEM(strip, F32),
@@ -539,12 +576,12 @@
             pltpu.VMEM((SWEEPS, along, 8, LANES), F32),
             pltpu.VMEM((8, LANES), F32),
             pltpu.VMEM((SURVEYS, rows), F32),
-            dma((4, tiles)),
+            dma((5, tiles)),
             dma((5, tiles)),
             dma((2,)),
             dma((2,)),
-            dma((SWEEPS, 2)),
-            dma((SWEEPS, 2)),
+            dma((SWEEPS + 1, 2)),
+            dma((SWEEPS + 1, 2)),
             dma((SWEEPS + 1,)),
             dma((SWEEPS + 1,)),
             dma((SWEEPS + 1,)),
@@ -558,11 +595,11 @@
                 jax.ShapeDtypeStruct((rows, cols), F32),
                 jax.ShapeDtypeStruct((SURVEYS, rows), F32),
             ),
-            in_specs=[pl.BlockSpec(memory_space=pl.ANY)] * 4 + [pl.BlockSpec(memory_space=pltpu.VMEM)],
+            in_specs=[pl.BlockSpec(memory_space=pl.ANY)] * 5,
             out_specs=(pl.BlockSpec(memory_space=pl.ANY), pl.BlockSpec(memory_space=pl.ANY)),
             scratch_shapes=scratch,
             compiler_params=pltpu.CompilerParams(
-                collective_id=0, has_side_effects=True, vmem_limit_bytes=60 * 1024 * 1024
+                collective_id=0, has_side_effects=True, vmem_limit_bytes=52 * 1024 * 1024
             ),
         )(heights, confidence, survey_ids, seam_mask, datum.reshape(1, SURVEYS))
 

time: 78.1 us -> 74.1 us (0.949)
  Pallas kernels: 74.4 us -> 71.1 us
    pallas_call x1, Pallas kernels: 74.4 us -> 71.1 us  [on_device(): pl.pallas_call(functools.partial(kernel, zsize, dims), out_shape=(jax.Sha...]
where the time goes in v3:
time: 74.1 us; the launch traced here: 74 us
  Pallas kernels  71.1 us (96%)
  local copies, waits for them, and re-layouts  2.26 us (3%)
    pallas_call x1, Pallas kernels, on_device(): pl.pallas_call(functools.partial(kernel, zsize, dims), out_shape=(jax.Sha...  71.1 us
    unnamed x4, local copies, waits for them, and re-layouts  2.26 us

profile of v3, /device:TPU:1, one launch (start us, length us, event | category | flops | bytes accessed | tf_op | source)
XLA Modules:
  0.0 74.0 jit_solution(2755384502445887706)
XLA Ops:
  0.6 0.0 copy-start
  0.6 0.6 copy-done
  1.3 71.1 %shard_map.68 = (f32[512,512]{1,0:T(8,128)S(1)}, f32[40,512]{1,0:T(8,128)S(1)}) custom-call(f32[512,512]{1,0:T(8,128)} %heights.1, f32[512,512]{1,0:T(8,128)} %confidence.1, s32[512,512]{1,0:T(8,128)} %survey_ids.1, s32[512,512]{1,0:T(8,128)} %seam_mask.1, f32[1,40]{1,0:T(1,128)S(1)} %bitcast.1), custom_call_target="tpu_custom_call" | custom-call | tf_op jit(solution)/shard_map/pallas_call | solution.py:592
  72.4 1.0 %copy.9 = f32[512,512]{1,0:T(8,128)} copy(f32[512,512]{1,0:T(8,128)S(1)} %get-tuple-element.4) | data formatting | bytes 2097152
  73.3 0.6 copy.10
Async XLA Ops:
  0.6 0.7 copy-start

commit v4 on v3

--- a/solution.py
+++ b/solution.py
@@ -15,6 +15,7 @@
 half_width = 0.95
 
 LANES = 128
+HIGH = 5
 DEPTH = 4
 MESH = pl.DeviceIdType.MESH
 F32 = jnp.float32
@@ -71,13 +72,20 @@
     strip_send,
     strip_recv,
     hist,
+    hist_first,
     parts,
+    parts_first,
     floor,
     zsend,
     zrecv,
     table,
     wtotal,
     offs,
+    row_cq,
+    row_ids,
+    base_send,
+    base_recv,
+    halo_table,
     load_sem,
     store_sem,
     strip_ss,
@@ -90,6 +98,8 @@
     z_rs,
     table_ss,
     table_rs,
+    halo_ss,
+    halo_rs,
 ):
     ny, nx, nc = dims
     along = ny * nx * nc
@@ -111,12 +121,13 @@
         a, b, c = step
         return (((-a) % ny) * nx + (-b) % nx) * nc + (-c) % nc
 
-    loads = []
-    for t in range(tiles):
+    loads = {}
+    load_order = [0, tiles - 1] + list(range(1, tiles - 1))
+    for t in load_order:
         for n, (src, dst) in enumerate(((survey_ids, ids), (confidence, cq), (heights, obs), (seam_mask, mask))):
             copy = pltpu.make_async_copy(src.at[:, pl.ds(t * LANES, LANES)], dst.at[t], load_sem.at[n, t])
             copy.start()
-            loads.append((n, copy))
+            loads[n, t] = copy
 
     datum_copy = pltpu.make_async_copy(datum, datum_row, load_sem.at[4, 0])
     datum_copy.start()
@@ -124,6 +135,10 @@
     mm[:, 0:8, :] = jnp.zeros((tiles + 1, 8, LANES), F32)
     mm[:, rows + 8 : rows + 16, :] = jnp.zeros((tiles + 1, 8, LANES), F32)
     strip_recv[...] = jnp.zeros(strip_recv.shape, F32)
+    row_cq[...] = jnp.zeros(row_cq.shape, F32)
+    row_ids[...] = jnp.zeros(row_ids.shape, I32)
+    base_recv[...] = jnp.zeros(base_recv.shape, F32)
+    halo_table[...] = jnp.zeros(halo_table.shape, F32)
 
     barrier = pltpu.get_barrier_semaphore()
     for step in steps:
@@ -131,9 +146,9 @@
     for k in range(1, zsize):
         pl.semaphore_signal(barrier, inc=1, device_id=((zi + k) % zsize, me), device_id_type=MESH)
 
-    for n, copy in loads:
-        if n < 3:
-            copy.wait()
+    for t in (0, tiles - 1):
+        for n in range(3):
+            loads[n, t].wait()
     datum_copy.wait()
     dat[...] = jnp.zeros((16, LANES), F32)
     dat[:, 0:SURVEYS] = jnp.broadcast_to(datum_row[...], (16, SURVEYS))
@@ -185,54 +200,63 @@
                 ]
                 onehot[g, r * 8 : r * 8 + 16, t * LANES : (t + 1) * LANES] = jnp.concatenate(pair, 0).astype(BF16)
 
-    def profile(values, hid, g):
-        high = values.astype(BF16)
-        low = (values - high.astype(F32)).astype(BF16)
-        zero = jnp.zeros_like(high)
-        match = [hid == h for h in range(5)]
-        left = jnp.concatenate([jnp.where(m, p, zero) for p in (high, low) for m in match], 0)
+    def profile(arrays, hid, g):
+        pieces = []
+        for values in arrays:
+            high = values.astype(BF16)
+            pieces += [high, (values - high.astype(F32)).astype(BF16)]
+        zero = jnp.zeros_like(pieces[0])
+        match = [hid == h for h in range(HIGH)]
+        left = jnp.concatenate([jnp.where(m, p, zero) for p in pieces for m in match], 0)
         full = lax.dot_general(left, onehot[g], (((1,), (1,)), ((), ())), preferred_element_type=F32)
         lane = lanes_of(8)
         sub = lax.broadcasted_iota(I32, (8, LANES), 0)
         own_row = (lane >> 3) & 7
         out = []
-        for j in range(2):
-            tile = jnp.zeros((8, LANES), F32)
-            for h in range(5):
-                value = 0.0
-                for part in range(2):
-                    at = (part * 5 + h) * 32 + 16 * j
-                    pair = [full[at + 8 * i : at + 8 * i + 8, j * LANES : (j + 1) * LANES] for i in range(2)]
-                    value += jnp.where(lane < 64, pair[0], pair[1])
-                value = jnp.take_along_axis(value, own_row, axis=0, mode="promise_in_bounds")
-                tile = jnp.where(sub == h, value, tile)
-            out.append(tile)
+        for n in range(len(arrays)):
+            for j in range(2):
+                tile = jnp.zeros((8, LANES), F32)
+                for h in range(HIGH):
+                    value = 0.0
+                    for part in range(2):
+                        at = ((2 * n + part) * HIGH + h) * 32 + 16 * j
+                        pair = [full[at + 8 * i : at + 8 * i + 8, j * LANES : (j + 1) * LANES] for i in range(2)]
+                        value += jnp.where(lane < 64, pair[0], pair[1])
+                    value = jnp.take_along_axis(value, own_row, axis=0, mode="promise_in_bounds")
+                    tile = jnp.where(sub == h, value, tile)
+                out.append(tile)
         return out
 
     def high_bits(r):
         return jnp.concatenate([(ids[t, r, :] >> 3) & 7 for t in range(tiles)], 1)
 
-    def put_profile(n, g, sums):
-        hist[n, 2 * g] = sums[0]
-        hist[n, 2 * g + 1] = sums[1]
-
-    def part_copy(n, step):
-        to = partner(step)
+    used = pl.ds(0, HIGH)
+
+    def put_profile(k, g, sums):
+        for j in range(2):
+            if k == 0:
+                hist_first[2 * g + j, 0] = sums[j]
+                hist_first[2 * g + j, 1] = sums[2 + j]
+            else:
+                hist[k, 2 * g + j] = sums[j]
+
+    def part_copy(k, to, slot):
         return pltpu.make_async_remote_copy(
-            hist.at[n, to],
-            parts.at[n, slot_of(step)],
-            part_ss.at[n],
-            part_rs.at[n],
+            hist_first.at[to, :, used] if k == 0 else hist.at[k, to, used],
+            parts_first.at[slot, :, used] if k == 0 else parts.at[k, slot, used],
+            part_ss.at[k],
+            part_rs.at[k],
             device_id=(zi, to),
             device_id_type=MESH,
         )
 
-    def all_parts(n):
+    def all_parts(k):
+        many = pl.ds(1, along - 1)
         return pltpu.make_async_remote_copy(
-            hist.at[n, pl.ds(1, along - 1)],
-            parts.at[n, pl.ds(1, along - 1)],
-            part_ss.at[n],
-            part_rs.at[n],
+            hist_first.at[many, :, used] if k == 0 else hist.at[k, many, used],
+            parts_first.at[many, :, used] if k == 0 else parts.at[k, many, used],
+            part_ss.at[k],
+            part_rs.at[k],
             device_id=(zi, me),
             device_id_type=MESH,
         )
@@ -257,61 +281,92 @@
             device_id_type=MESH,
         )
 
-    def send_profile(n):
-        total = jnp.sum(hist[n], axis=0)
+    def send_total(n, total):
         zsend[n] = total
         zrecv[n, 0] = total
         for k in sorted(range(1, zsize), key=lambda k: -torus_distance(k, zsize)):
             z_copy(n, k).start()
+
+    def send_inner(k):
         for step in steps:
-            part_copy(n, step).start()
-        parts[n, 0] = hist[n, me]
-
-    def summed_parts(n):
-        all_parts(n).wait_recv()
-        return jnp.sum(parts[n], axis=0)
+            to = partner(step)
+
+            @pl.when((to >= 2) & (to < along - 2))
+            def _():
+                part_copy(k, to, slot_of(step)).start()
+
+    def send_outer(k):
+        for to in (0, 1, along - 2, along - 1):
+            y, x, c = to // (nx * nc), (to // nc) % nx, to % nc
+            slot = (((my_y + ny - y) % ny) * nx + (my_x + nx - x) % nx) * nc + (my_c + nc - c) % nc
+
+            @pl.when(me != to)
+            def _():
+                part_copy(k, to, slot).start()
+
+        if k == 0:
+            parts_first[0, :, 0:HIGH, :] = hist_first[me, :, 0:HIGH, :]
+            send_total(0, jnp.sum(hist_first[:, 0], axis=0))
+            send_total(SWEEPS, jnp.sum(hist_first[:, 1], axis=0))
+        else:
+            parts[k, 0, 0:HIGH, :] = hist[k, me, 0:HIGH, :]
+            send_total(k, jnp.sum(hist[k], axis=0))
 
     def summed_z(n):
         all_z(n).wait_recv()
         return jnp.broadcast_to(jnp.sum(jnp.sum(zrecv[n], axis=0), keepdims=True), (8, LANES))
 
-    for n, copy in loads:
-        if n == 3:
-            copy.wait()
-
-    def row_copy(k, n, side):
-        at, to = ((8, rows + 8), (rows + 7, 7))[side]
-        which = pl.ds(0, tiles) if n == SWEEPS else pl.ds(tiles, 1) if k == 0 else pl.ds(0, tiles + 1)
-        return pltpu.make_async_remote_copy(
-            mm.at[which, pl.ds(at, 1), :],
-            mm.at[which, pl.ds(to, 1), :],
-            row_ss.at[n, side],
-            row_rs.at[n, side],
-            device_id=(zi - 1 if side == 0 else zi + 1, me),
-            device_id_type=MESH,
-        )
-
     above = (zi > 0, zi < zsize - 1)
 
-    def send_rows(k, n):
+    def row_copies(n, side):
+        own, far = ((0, rows + 8), (rows - 8, 0))[side]
+        own, far, shifted = pl.ds(own, 8), pl.ds(far, 8), pl.ds(own + 8, 8)
+        every = pl.ds(0, tiles + 1)
+        if n == 0:
+            pairs = [(mm.at[pl.ds(0, tiles), shifted, :], mm.at[pl.ds(0, tiles), far, :])]
+        elif n == 1:
+            pairs = [
+                (mm.at[pl.ds(tiles, 1), shifted, :], mm.at[pl.ds(tiles, 1), far, :]),
+                (cq.at[every, own, :], row_cq.at[1 - side]),
+                (ids.at[every, own, :], row_ids.at[1 - side]),
+            ]
+        else:
+            pairs = [(base_send.at[n - 2, side], base_recv.at[n - 2, 1 - side])]
+        return [
+            pltpu.make_async_remote_copy(
+                src,
+                dst,
+                row_ss.at[n, side, i],
+                row_rs.at[n, side, i],
+                device_id=(zi - 1 if side == 0 else zi + 1, me),
+                device_id_type=MESH,
+            )
+            for i, (src, dst) in enumerate(pairs)
+        ]
+
+    def send_rows(n):
         for side in range(2):
 
             @pl.when(above[side])
             def _():
-                row_copy(k, n, side).start()
-
-    def wait_rows(k, n):
+                for copy in row_copies(n, side):
+                    copy.start()
+
+    def wait_rows(n):
         for side in range(2):
 
             @pl.when(above[1 - side])
             def _():
-                row_copy(k, n, side).wait_recv()
-
+                for copy in row_copies(n, side):
+                    copy.wait_recv()
+
+    def rows_sent(n):
         for side in range(2):
 
             @pl.when(above[side])
             def _():
-                row_copy(k, n, side).wait_send()
+                for copy in row_copies(n, side):
+                    copy.wait_send()
 
     def prepare(g, t):
         r = pl.ds(pl.multiple_of(g * 32, 32), 32)
@@ -325,6 +380,8 @@
             seen = jnp.where(inside, seen, 0.0)
             inverse = jnp.where(inside, inverse, 0.0)
         share = weight * inverse
+        if t < tiles:
+            w[t, r, :] = weight
         ids[t, r, :] = survey + upper
         obs[t, r, :] = seen
         q[t, r, :] = inverse
@@ -332,22 +389,19 @@
         pp[t, r, :] = share * seen
         mm[t, pl.ds(pl.multiple_of(g * 32 + 8, 8), 32), :] = seen
 
-    def start_group(g, _):
-        r = pl.ds(pl.multiple_of(g * 32, 32), 32)
-        make_onehot(g)
-        values = []
-        for t in range(tiles):
-            value = mask[t, r, :].astype(F32) * cq[t, r, :]
-            w[t, r, :] = value
-            values.append(value)
-        put_profile(SWEEPS, g, profile(jnp.concatenate(values, 1), high_bits(r), g))
-        for t in range(tiles):
+    for t in load_order:
+
+        def start_group(g, _, t=t):
             prepare(g, t)
-        return 0
-
-    lax.fori_loop(0, groups, start_group, 0, unroll=4)
-    send_rows(0, SWEEPS)
-    send_profile(SWEEPS)
+            return 0
+
+        for n in range(3):
+            if t not in (0, tiles - 1):
+                loads[n, t].wait()
+        lax.fori_loop(0, groups, start_group, 0, unroll=8)
+    send_rows(0)
+    for t in range(tiles):
+        loads[3, t].wait()
 
     for side in range(2):
 
@@ -373,15 +427,15 @@
         prepare(g, tiles)
         return 0
 
-    lax.fori_loop(0, groups, unpack_strip, 0, unroll=4)
-    send_rows(0, 0)
+    lax.fori_loop(0, groups, unpack_strip, 0, unroll=8)
+    send_rows(1)
 
     def stencil_group(k, g):
         first = g * 32
         r = pl.ds(pl.multiple_of(first, 32), 32)
         lane = lanes_of(32)
         now = [mm[t, pl.ds(pl.multiple_of(first + 8, 8), 32), :] for t in range(tiles + 1)]
-        gaps = []
+        gaps, weights = [], []
         for t in range(tiles + 1):
             before, after = now[(t - 1) % (tiles + 1)], now[(t + 1) % (tiles + 1)]
             value = mm[t, pl.ds(first + 7, 32), :] + mm[t, pl.ds(first + 9, 32), :]
@@ -389,8 +443,16 @@
             value += pltpu.roll(jnp.where(lane == 0, after, now[t]), LANES - 1, 1)
             bes[t, r, :] = value
             if t < tiles:
+                if k == 0:
+                    weight = mask[t, r, :].astype(F32) * w[t, r, :]
+                    w[t, r, :] = weight
+                    weights.append(weight)
                 gaps.append(w[t, r, :] * (0.25 * value - obs[t, r, :]))
-        put_profile(k, g, profile(jnp.concatenate(gaps, 1), high_bits(r), g))
+        arrays = [jnp.concatenate(gaps, 1)]
+        if k == 0:
+            make_onehot(g)
+            arrays.append(jnp.concatenate(weights, 1))
+        put_profile(k, g, profile(arrays, high_bits(r), g))
 
     def local_update(k, alpha, beta):
         def block(b, _):
@@ -409,47 +471,102 @@
         gap_total = summed_z(k)
         if k == 0:
             weight_total = summed_z(SWEEPS)
-            floor[...] = 1.0 / jnp.maximum(summed_parts(SWEEPS), 1.0)
-        share = summed_parts(k) * floor[...]
+            all_parts(0).wait_recv()
+            floor[...] = 1.0 / jnp.maximum(jnp.sum(parts_first[:, 1, 0:HIGH, :], axis=0), 1.0)
+            share = jnp.sum(parts_first[:, 0, 0:HIGH, :], axis=0) * floor[...]
+        else:
+            all_parts(k).wait_recv()
+            share = jnp.sum(parts[k, :, 0:HIGH, :], axis=0) * floor[...]
         lane = lanes_of(8)
         sub = lax.broadcasted_iota(I32, (8, LANES), 0)
         index = 8 * (sub + jnp.where(lane >= 64, 8, 0)) + (lane & 7)
         kind = (lane & 63) >> 3
         tile = jnp.zeros((8, LANES), F32)
-        for h in range(5):
+        for h in range(HIGH):
             tile = jnp.where(kind == h, lane_take(jnp.broadcast_to(share[h : h + 1], (8, LANES)), index), tile)
         tile = jnp.where(kind == 5, gap_total, tile)
         if k == 0:
             tile = jnp.where(kind > 5, weight_total, tile)
         table[k, me] = tile
 
+    kind = jnp.where(me == 0, 1, jnp.where(me == along - 1, 2, 0))
+    enders = (me == 0, me == along - 1)
+
     def table_copy(k, step):
         return pltpu.make_async_remote_copy(
             table.at[k, me],
             table.at[k, me],
             table_ss.at[k],
-            table_rs.at[k],
+            table_rs.at[k, kind],
             device_id=(zi, partner(step)),
             device_id_type=MESH,
         )
 
-    def all_table(k):
+    def some_table(k, count, which):
         return pltpu.make_async_remote_copy(
-            table.at[k, pl.ds(0, along - 1)],
-            table.at[k, pl.ds(0, along - 1)],
+            table.at[k, pl.ds(0, count)],
+            table.at[k, pl.ds(0, count)],
             table_ss.at[k],
-            table_rs.at[k],
+            table_rs.at[k, which],
             device_id=(zi, me),
             device_id_type=MESH,
         )
+
+    def hand_on(k, side):
+        return pltpu.make_async_remote_copy(
+            table.at[k, 0 if side == 0 else along - 1],
+            halo_table.at[k, 1 - side],
+            halo_ss.at[k, side],
+            halo_rs.at[k, 1 - side],
+            device_id=(zi - 1 if side == 0 else zi + 1, me),
+            device_id_type=MESH,
+        )
+
+    def receive_tables(k, last):
+        for side in range(2):
+
+            @pl.when(jnp.logical_not(enders[side]))
+            def _():
+                some_table(k, 1, 1 + side).wait_recv()
+
+            if not last:
+
+                @pl.when(above[side])
+                def _():
+                    hand_on(k, side).start()
+
+        ender = enders[0] | enders[1]
+
+        @pl.when(ender)
+        def _():
+            some_table(k, along - 2, 0).wait_recv()
+
+        @pl.when(jnp.logical_not(ender))
+        def _():
+            some_table(k, along - 2 - 1, 0).wait_recv()
+
+    def update_halo(k, beta, level):
+        wait_rows(k + 2)
+        for side in range(2):
+
+            @pl.when(above[side])
+            def _():
+                hand_on(k, 1 - side).wait_recv()
+
+            row_table = halo_table[k, side]
+            at = (0, rows + 8)[side]
+            for t in range(tiles + 1):
+                step = beta * row_cq[side, t] * (lane_take(row_table, row_ids[side, t]) - level[:8])
+                mm[t, at : at + 8, :] = base_recv[k, side, t] + step
 
     def update_group(g, beta, level, last):
         r = pl.ds(pl.multiple_of(g * 32, 32), 32)
         at = pl.ds(pl.multiple_of(g * 32 + 8, 8), 32)
         row_table = [table[last, 2 * g + i] for i in (0, 0, 1, 1)]
-        row_table = jnp.concatenate(row_table, 0) - level
+        row_table = jnp.concatenate(row_table, 0)
         for t in range(tiles if last == SWEEPS - 1 else tiles + 1):
-            step = d[t, r, :] + beta * cq[t, r, :] * lane_take(row_table, ids[t, r, :])
+            spread = lane_take(row_table, ids[t, r, :]) - level
+            step = d[t, r, :] + beta * cq[t, r, :] * spread
             if last < SWEEPS - 1:
                 d[t, r, :] = step
             mm[t, at, :] = mm[t, at, :] + step
@@ -457,6 +574,7 @@
     stores = []
     level, before = None, None
     for k, (alpha, beta) in enumerate(coefficients()):
+        last = k == SWEEPS - 1
         if k == 0:
 
             def first(g, _):
@@ -464,12 +582,13 @@
                 return 0
 
             lax.fori_loop(1, groups - 1, first, 0, unroll=14)
-            wait_rows(0, SWEEPS)
-            wait_rows(0, 0)
+            send_inner(0)
+            for n in range(2):
+                wait_rows(n)
+            for n in range(2):
+                rows_sent(n)
         else:
             update_group(0, before, level, k - 1)
-            update_group(groups - 1, before, level, k - 1)
-            send_rows(k, k)
             update_group(1, before, level, k - 1)
 
             def both(g, _, k=k, before=before, level=level):
@@ -477,18 +596,23 @@
                 stencil_group(k, g)
                 return 0
 
-            lax.fori_loop(1, groups - 2, both, 0, unroll=13)
-            stencil_group(k, groups - 2)
-            wait_rows(k, k)
+            lax.fori_loop(1, groups - 1, both, 0, unroll=14)
+            send_inner(k)
+            update_halo(k - 1, before, level)
         stencil_group(k, 0)
         stencil_group(k, groups - 1)
-        send_profile(k)
+        send_outer(k)
         local_update(k, alpha, beta)
+        if not last:
+            for side, at in enumerate((0, rows - 8)):
+                for t in range(tiles + 1):
+                    base_send[k, side, t] = mm[t, at + 8 : at + 16, :] + d[t, at : at + 8, :]
+            send_rows(k + 2)
 
         owner_tile(k)
         for step in steps:
             table_copy(k, step).start()
-        all_table(k).wait_recv()
+        receive_tables(k, last)
 
         whole = jnp.sum(table[k], axis=0)
         if k == 0:
@@ -531,10 +655,18 @@
             strip_copy(side).wait_send()
 
     for n in range(SWEEPS + 1):
-        all_parts(n).wait_send()
         all_z(n).wait_send()
     for k in range(SWEEPS):
-        all_table(k).wait_send()
+        all_parts(k).wait_send()
+        some_table(k, along - 1, 0).wait_send()
+    for k in range(SWEEPS - 1):
+        rows_sent(k + 2)
+        for side in range(2):
+
+            @pl.when(above[side])
+            def _():
+                hand_on(k, side).wait_send()
+
     for copy in stores:
         copy.wait()
 
@@ -568,26 +700,35 @@
             pltpu.VMEM((16, LANES), F32),
             pltpu.VMEM(strip, F32),
             pltpu.VMEM(strip, F32),
-            pltpu.VMEM((SWEEPS + 1, along, 8, LANES), F32),
-            pltpu.VMEM((SWEEPS + 1, along, 8, LANES), F32),
-            pltpu.VMEM((8, LANES), F32),
+            pltpu.VMEM((SWEEPS, along, 8, LANES), F32),
+            pltpu.VMEM((along, 2, 8, LANES), F32),
+            pltpu.VMEM((SWEEPS, along, 8, LANES), F32),
+            pltpu.VMEM((along, 2, 8, LANES), F32),
+            pltpu.VMEM((HIGH, LANES), F32),
             pltpu.VMEM((SWEEPS + 1, 8, LANES), F32),
             pltpu.VMEM((SWEEPS + 1, zsize, 8, LANES), F32),
             pltpu.VMEM((SWEEPS, along, 8, LANES), F32),
             pltpu.VMEM((8, LANES), F32),
             pltpu.VMEM((SURVEYS, rows), F32),
+            pltpu.VMEM((2, tiles + 1, 8, LANES), F32),
+            pltpu.VMEM((2, tiles + 1, 8, LANES), I32),
+            pltpu.VMEM((SWEEPS - 1, 2, tiles + 1, 8, LANES), F32),
+            pltpu.VMEM((SWEEPS - 1, 2, tiles + 1, 8, LANES), F32),
+            pltpu.VMEM((SWEEPS - 1, 2, 8, LANES), F32),
             dma((5, tiles)),
             dma((5, tiles)),
             dma((2,)),
             dma((2,)),
-            dma((SWEEPS + 1, 2)),
-            dma((SWEEPS + 1, 2)),
-            dma((SWEEPS + 1,)),
-            dma((SWEEPS + 1,)),
+            dma((SWEEPS + 1, 2, 3)),
+            dma((SWEEPS + 1, 2, 3)),
+            dma((SWEEPS,)),
+            dma((SWEEPS,)),
             dma((SWEEPS + 1,)),
             dma((SWEEPS + 1,)),
             dma((SWEEPS,)),
-            dma((SWEEPS,)),
+            dma((SWEEPS, 3)),
+            dma((SWEEPS - 1, 2)),
+            dma((SWEEPS - 1, 2)),
         ]
         return pl.pallas_call(
             functools.partial(kernel, zsize, dims),

time: 74.1 us -> 73.1 us (0.987)
  Pallas kernels: 71.1 us -> 70.2 us
    pallas_call x1, Pallas kernels: 71.1 us -> 70.2 us  [on_device(): pl.pallas_call(functools.partial(kernel, zsize, dims), out_shape=(jax.Sha...]
where the time goes in v4:
time: 73.1 us
  Pallas kernels  70.2 us (96%)
  local copies, waits for them, and re-layouts  2.26 us (3%)
    pallas_call x1, Pallas kernels, on_device(): pl.pallas_call(functools.partial(kernel, zsize, dims), out_shape=(jax.Sha...  70.2 us
    unnamed x4, local copies, waits for them, and re-layouts  2.26 us

profile of v4, /device:TPU:1, one launch (start us, length us, event | category | flops | bytes accessed | tf_op | source)
XLA Modules:
  0.0 73.1 jit_solution(18408719038163514073)
XLA Ops:
  0.6 0.0 copy-start
  0.6 0.6 copy-done
  1.3 70.2 %shard_map.68 = (f32[512,512]{1,0:T(8,128)S(1)}, f32[40,512]{1,0:T(8,128)S(1)}) custom-call(f32[512,512]{1,0:T(8,128)} %heights.1, f32[512,512]{1,0:T(8,128)} %confidence.1, s32[512,512]{1,0:T(8,128)} %survey_ids.1, s32[512,512]{1,0:T(8,128)} %seam_mask.1, f32[1,40]{1,0:T(1,128)S(1)} %bitcast.1), custom_call_target="tpu_custom_call" | custom-call | tf_op jit(solution)/shard_map/pallas_call | solution.py:733
  71.4 1.0 %copy.9 = f32[512,512]{1,0:T(8,128)} copy(f32[512,512]{1,0:T(8,128)S(1)} %get-tuple-element.4) | data formatting | bytes 2097152
  72.4 0.6 copy.10
Async XLA Ops:
  0.6 0.7 copy-start

commit v5 on v4

--- a/solution.py
+++ b/solution.py
@@ -86,6 +86,9 @@
     base_send,
     base_recv,
     halo_table,
+    extra,
+    extra_first,
+    extra_floor,
     load_sem,
     store_sem,
     strip_ss,
@@ -100,6 +103,8 @@
     table_rs,
     halo_ss,
     halo_rs,
+    extra_ss,
+    extra_rs,
 ):
     ny, nx, nc = dims
     along = ny * nx * nc
@@ -113,9 +118,14 @@
     steps = [(a, b, c) for a in range(ny) for b in range(nx) for c in range(nc)]
     steps = sorted(steps[1:], key=lambda s: -(torus_distance(s[0], ny) + torus_distance(s[1], nx) + 0.3 * s[2]))
 
+    def turned(value, size):
+        return [jnp.where(value + a >= size, value + a - size, value + a) for a in range(size)]
+
+    ys, xs, cs = turned(my_y, ny), turned(my_x, nx), turned(my_c, nc)
+    partners = {(a, b, c): (ys[a] * nx + xs[b]) * nc + cs[c] for a, b, c in [(0, 0, 0)] + steps}
+
     def partner(step):
-        a, b, c = step
-        return (((my_y + a) % ny) * nx + (my_x + b) % nx) * nc + (my_c + c) % nc
+        return partners[step]
 
     def slot_of(step):
         a, b, c = step
@@ -145,6 +155,16 @@
         pl.semaphore_signal(barrier, inc=1, device_id=(zi, partner(step)), device_id_type=MESH)
     for k in range(1, zsize):
         pl.semaphore_signal(barrier, inc=1, device_id=((zi + k) % zsize, me), device_id_type=MESH)
+
+    for side in range(2):
+        inside = zi > 0 if side == 0 else zi < zsize - 1
+
+        @pl.when(inside & (me == (0 if side == 0 else along - 1)))
+        def _():
+            for step in steps:
+                to = (zi - 1 if side == 0 else zi + 1, partner(step))
+                pl.semaphore_signal(barrier, inc=1, device_id=to, device_id_type=MESH)
+
 
     for t in (0, tiles - 1):
         for n in range(3):
@@ -169,7 +189,9 @@
     for b in range(rows // span):
         strip_send[b] = bes[0, b * span : (b + 1) * span, :].T
 
-    pl.semaphore_wait(barrier, along + zsize - 2)
+    greeted = jnp.where((zi > 0) & (me != along - 1), 1, 0) + jnp.where((zi < zsize - 1) & (me != 0), 1, 0)
+    pl.semaphore_wait(barrier, along + zsize - 2 + greeted)
+
 
     def strip_copy(side):
         at = pl.ds(0, 16) if side == 0 else pl.ds(112, 16)
@@ -400,6 +422,11 @@
                 loads[n, t].wait()
         lax.fori_loop(0, groups, start_group, 0, unroll=8)
     send_rows(0)
+    def own_onehot(g, _):
+        make_onehot(g)
+        return 0
+
+    lax.fori_loop(0, groups, own_onehot, 0, unroll=8)
     for t in range(tiles):
         loads[3, t].wait()
 
@@ -408,9 +435,6 @@
         @pl.when(has[1 - side])
         def _():
             strip_copy(side).wait_recv()
-
-    for b in range(rows // span):
-        bes[0, b * span : (b + 1) * span, :] = strip_recv[b].T
 
     def unpack_strip(g, _):
         r = pl.ds(pl.multiple_of(g * 32, 32), 32)
@@ -427,8 +451,15 @@
         prepare(g, tiles)
         return 0
 
-    lax.fori_loop(0, groups, unpack_strip, 0, unroll=8)
-    send_rows(1)
+    blocks = rows // span
+    order = [0, blocks - 1] + list(range(1, blocks - 1)) if blocks > 1 else [0]
+    for i, b in enumerate(order):
+        bes[0, b * span : (b + 1) * span, :] = strip_recv[b].T
+        if i == min(1, blocks - 1):
+            unpack_strip(0, 0)
+            unpack_strip(groups - 1, 0)
+            send_rows(1)
+    lax.fori_loop(1, groups - 1, unpack_strip, 0, unroll=7)
 
     def stencil_group(k, g):
         first = g * 32
@@ -450,7 +481,6 @@
                 gaps.append(w[t, r, :] * (0.25 * value - obs[t, r, :]))
         arrays = [jnp.concatenate(gaps, 1)]
         if k == 0:
-            make_onehot(g)
             arrays.append(jnp.concatenate(weights, 1))
         put_profile(k, g, profile(arrays, high_bits(r), g))
 
@@ -467,6 +497,16 @@
 
         lax.fori_loop(0, rows // 32, block, 0, unroll=4)
 
+    def row_tile(share):
+        lane = lanes_of(8)
+        sub = lax.broadcasted_iota(I32, (8, LANES), 0)
+        index = 8 * (sub + jnp.where(lane >= 64, 8, 0)) + (lane & 7)
+        kind = (lane & 63) >> 3
+        tile = jnp.zeros((8, LANES), F32)
+        for h in range(HIGH):
+            tile = jnp.where(kind == h, lane_take(jnp.broadcast_to(share[h : h + 1], (8, LANES)), index), tile)
+        return tile
+
     def owner_tile(k):
         gap_total = summed_z(k)
         if k == 0:
@@ -477,73 +517,98 @@
         else:
             all_parts(k).wait_recv()
             share = jnp.sum(parts[k, :, 0:HIGH, :], axis=0) * floor[...]
-        lane = lanes_of(8)
-        sub = lax.broadcasted_iota(I32, (8, LANES), 0)
-        index = 8 * (sub + jnp.where(lane >= 64, 8, 0)) + (lane & 7)
-        kind = (lane & 63) >> 3
-        tile = jnp.zeros((8, LANES), F32)
-        for h in range(HIGH):
-            tile = jnp.where(kind == h, lane_take(jnp.broadcast_to(share[h : h + 1], (8, LANES)), index), tile)
+        kind = (lanes_of(8) & 63) >> 3
+        tile = row_tile(share)
         tile = jnp.where(kind == 5, gap_total, tile)
         if k == 0:
             tile = jnp.where(kind > 5, weight_total, tile)
         table[k, me] = tile
 
-    kind = jnp.where(me == 0, 1, jnp.where(me == along - 1, 2, 0))
-    enders = (me == 0, me == along - 1)
-
     def table_copy(k, step):
         return pltpu.make_async_remote_copy(
             table.at[k, me],
             table.at[k, me],
             table_ss.at[k],
-            table_rs.at[k, kind],
+            table_rs.at[k],
             device_id=(zi, partner(step)),
             device_id_type=MESH,
         )
 
-    def some_table(k, count, which):
-        return pltpu.make_async_remote_copy(
-            table.at[k, pl.ds(0, count)],
-            table.at[k, pl.ds(0, count)],
+    def all_table(k):
+        return pltpu.make_async_remote_copy(
+            table.at[k, pl.ds(0, along - 1)],
+            table.at[k, pl.ds(0, along - 1)],
             table_ss.at[k],
-            table_rs.at[k, which],
+            table_rs.at[k],
             device_id=(zi, me),
             device_id_type=MESH,
         )
 
-    def hand_on(k, side):
-        return pltpu.make_async_remote_copy(
-            table.at[k, 0 if side == 0 else along - 1],
-            halo_table.at[k, 1 - side],
+    enders = (me == 0, me == along - 1)
+
+    def extra_copy(k, side):
+        tile = 0 if side == 0 else along - 1
+        return pltpu.make_async_remote_copy(
+            hist_first.at[tile, :, used] if k == 0 else hist.at[k, tile, used],
+            extra_first.at[1 - side, me, :, used] if k == 0 else extra.at[k, 1 - side, me, used],
+            extra_ss.at[k, side],
+            extra_rs.at[k, 1 - side],
+            device_id=(zi - 1 if side == 0 else zi + 1, along - 1 if side == 0 else 0),
+            device_id_type=MESH,
+        )
+
+    def send_extra(k):
+        for side in range(2):
+
+            @pl.when(above[side])
+            def _():
+                extra_copy(k, side).start()
+
+    def all_extra(k, side):
+        return pltpu.make_async_remote_copy(
+            hist_first.at[:, :, used] if k == 0 else hist.at[k, :, used],
+            extra_first.at[side, :, :, used] if k == 0 else extra.at[k, side, :, used],
+            extra_ss.at[k, side],
+            extra_rs.at[k, side],
+            device_id=(zi, me),
+            device_id_type=MESH,
+        )
+
+    def halo_table_copy(k, side, step):
+        return pltpu.make_async_remote_copy(
+            halo_table.at[k, side],
+            halo_table.at[k, side],
             halo_ss.at[k, side],
-            halo_rs.at[k, 1 - side],
-            device_id=(zi - 1 if side == 0 else zi + 1, me),
-            device_id_type=MESH,
-        )
-
-    def receive_tables(k, last):
+            halo_rs.at[k, side],
+            device_id=(zi, partner(step)),
+            device_id_type=MESH,
+        )
+
+    def all_halo_table(k, side):
+        return pltpu.make_async_remote_copy(
+            table.at[k, pl.ds(0, along - 1)],
+            table.at[k, pl.ds(0, along - 1)],
+            halo_ss.at[k, side],
+            halo_rs.at[k, side],
+            device_id=(zi, me),
+            device_id_type=MESH,
+        )
+
+    def extra_tiles(k):
         for side in range(2):
 
-            @pl.when(jnp.logical_not(enders[side]))
-            def _():
-                some_table(k, 1, 1 + side).wait_recv()
-
-            if not last:
-
-                @pl.when(above[side])
-                def _():
-                    hand_on(k, side).start()
-
-        ender = enders[0] | enders[1]
-
-        @pl.when(ender)
-        def _():
-            some_table(k, along - 2, 0).wait_recv()
-
-        @pl.when(jnp.logical_not(ender))
-        def _():
-            some_table(k, along - 2 - 1, 0).wait_recv()
+            @pl.when(above[side] & enders[side])
+            def _():
+                all_extra(k, side).wait_recv()
+                if k == 0:
+                    total = jnp.sum(extra_first[side, :, 1, 0:HIGH, :], axis=0)
+                    extra_floor[...] = 1.0 / jnp.maximum(total, 1.0)
+                    share = jnp.sum(extra_first[side, :, 0, 0:HIGH, :], axis=0)
+                else:
+                    share = jnp.sum(extra[k, side, :, 0:HIGH, :], axis=0)
+                halo_table[k, side] = row_tile(share * extra_floor[...])
+                for step in steps:
+                    halo_table_copy(k, side, step).start()
 
     def update_halo(k, beta, level):
         wait_rows(k + 2)
@@ -551,7 +616,10 @@
 
             @pl.when(above[side])
             def _():
-                hand_on(k, 1 - side).wait_recv()
+                @pl.when(jnp.logical_not(enders[side]))
+                def _():
+                    halo_table_copy(k, side, (0, 0, 0)).wait_recv()
+
 
             row_table = halo_table[k, side]
             at = (0, rows + 8)[side]
@@ -601,6 +669,8 @@
             update_halo(k - 1, before, level)
         stencil_group(k, 0)
         stencil_group(k, groups - 1)
+        if not last:
+            send_extra(k)
         send_outer(k)
         local_update(k, alpha, beta)
         if not last:
@@ -612,7 +682,9 @@
         owner_tile(k)
         for step in steps:
             table_copy(k, step).start()
-        receive_tables(k, last)
+        if not last:
+            extra_tiles(k)
+        all_table(k).wait_recv()
 
         whole = jnp.sum(table[k], axis=0)
         if k == 0:
@@ -622,6 +694,16 @@
         before = beta
 
     chunks = 4
+    for b in range(rows // span):
+        pieces = []
+        for o in range(b * span // 16, (b + 1) * span // 16):
+            piece = table[SWEEPS - 1, o] - level[:8]
+            pieces += [piece, pltpu.roll(piece, 64, 1)]
+        offs[:, b * span : (b + 1) * span] = jnp.concatenate(pieces, 0).T[:SURVEYS]
+    copy = pltpu.make_async_copy(offs, offsets_out, store_sem.at[chunks, 0])
+    copy.start()
+    stores.append(copy)
+
     for c in range(chunks):
         size = rows // chunks
 
@@ -638,16 +720,6 @@
             )
             copy.start()
             stores.append(copy)
-    for b in range(rows // span):
-        pieces = []
-        for o in range(b * span // 16, (b + 1) * span // 16):
-            piece = table[SWEEPS - 1, o] - level[:8]
-            pieces += [piece, pltpu.roll(piece, 64, 1)]
-        offs[:, b * span : (b + 1) * span] = jnp.concatenate(pieces, 0).T[:SURVEYS]
-    copy = pltpu.make_async_copy(offs, offsets_out, store_sem.at[chunks, 0])
-    copy.start()
-    stores.append(copy)
-
     for side in range(2):
 
         @pl.when(has[side])
@@ -658,14 +730,18 @@
         all_z(n).wait_send()
     for k in range(SWEEPS):
         all_parts(k).wait_send()
-        some_table(k, along - 1, 0).wait_send()
+        all_table(k).wait_send()
     for k in range(SWEEPS - 1):
         rows_sent(k + 2)
         for side in range(2):
 
             @pl.when(above[side])
             def _():
-                hand_on(k, side).wait_send()
+                extra_copy(k, side).wait_send()
+
+            @pl.when(above[side] & enders[side])
+            def _():
+                all_halo_table(k, side).wait_send()
 
     for copy in stores:
         copy.wait()
@@ -715,6 +791,9 @@
             pltpu.VMEM((SWEEPS - 1, 2, tiles + 1, 8, LANES), F32),
             pltpu.VMEM((SWEEPS - 1, 2, tiles + 1, 8, LANES), F32),
             pltpu.VMEM((SWEEPS - 1, 2, 8, LANES), F32),
+            pltpu.VMEM((SWEEPS - 1, 2, along, 8, LANES), F32),
+            pltpu.VMEM((2, along, 2, 8, LANES), F32),
+            pltpu.VMEM((HIGH, LANES), F32),
             dma((5, tiles)),
             dma((5, tiles)),
             dma((2,)),
@@ -726,7 +805,9 @@
             dma((SWEEPS + 1,)),
             dma((SWEEPS + 1,)),
             dma((SWEEPS,)),
-            dma((SWEEPS, 3)),
+            dma((SWEEPS,)),
+            dma((SWEEPS - 1, 2)),
+            dma((SWEEPS - 1, 2)),
             dma((SWEEPS - 1, 2)),
             dma((SWEEPS - 1, 2)),
         ]

time: 73.1 us -> 72.1 us (0.986)
  Pallas kernels: 70.2 us -> 69.1 us
    pallas_call x1, Pallas kernels: 70.2 us -> 69.1 us  [on_device(): pl.pallas_call(functools.partial(kernel, zsize, dims), out_shape=(jax.Sha...]
where the time goes in v5:
time: 72.1 us; the launch traced here: 72 us
  Pallas kernels  69.1 us (96%)
  local copies, waits for them, and re-layouts  2.26 us (3%)
    pallas_call x1, Pallas kernels, on_device(): pl.pallas_call(functools.partial(kernel, zsize, dims), out_shape=(jax.Sha...  69.1 us
    unnamed x4, local copies, waits for them, and re-layouts  2.26 us

profile of v5, /device:TPU:1, one launch (start us, length us, event | category | flops | bytes accessed | tf_op | source)
XLA Modules:
  0.0 72.0 jit_solution(1879724577168408164)
XLA Ops:
  0.6 0.0 copy-start
  0.6 0.6 copy-done
  1.3 69.1 %shard_map.68 = (f32[512,512]{1,0:T(8,128)S(1)}, f32[40,512]{1,0:T(8,128)S(1)}) custom-call(f32[512,512]{1,0:T(8,128)} %heights.1, f32[512,512]{1,0:T(8,128)} %confidence.1, s32[512,512]{1,0:T(8,128)} %survey_ids.1, s32[512,512]{1,0:T(8,128)} %seam_mask.1, f32[1,40]{1,0:T(1,128)S(1)} %bitcast.1), custom_call_target="tpu_custom_call" | custom-call | tf_op jit(solution)/shard_map/pallas_call | solution.py:814
  70.4 1.0 %copy.9 = f32[512,512]{1,0:T(8,128)} copy(f32[512,512]{1,0:T(8,128)S(1)} %get-tuple-element.4) | data formatting | bytes 2097152
  71.4 0.6 copy.10
Async XLA Ops:
  0.6 0.7 copy-start

commit v6 on v5

--- a/solution.py
+++ b/solution.py
@@ -133,11 +133,15 @@
 
     loads = {}
     load_order = [0, tiles - 1] + list(range(1, tiles - 1))
+    def load(n, t):
+        src, dst = ((survey_ids, ids), (confidence, cq), (heights, obs), (seam_mask, mask))[n]
+        copy = pltpu.make_async_copy(src.at[:, pl.ds(t * LANES, LANES)], dst.at[t], load_sem.at[n, t])
+        copy.start()
+        loads[n, t] = copy
+
     for t in load_order:
-        for n, (src, dst) in enumerate(((survey_ids, ids), (confidence, cq), (heights, obs), (seam_mask, mask))):
-            copy = pltpu.make_async_copy(src.at[:, pl.ds(t * LANES, LANES)], dst.at[t], load_sem.at[n, t])
-            copy.start()
-            loads[n, t] = copy
+        for n in range(3):
+            load(n, t)
 
     datum_copy = pltpu.make_async_copy(datum, datum_row, load_sem.at[4, 0])
     datum_copy.start()
@@ -166,6 +170,8 @@
                 pl.semaphore_signal(barrier, inc=1, device_id=to, device_id_type=MESH)
 
 
+    for t in range(tiles):
+        load(3, t)
     for t in (0, tiles - 1):
         for n in range(3):
             loads[n, t].wait()
@@ -688,12 +694,12 @@
 
         whole = jnp.sum(table[k], axis=0)
         if k == 0:
-            wtotal[...] = lane_take(whole, jnp.full((8, LANES), 48, I32)) + 1.0
-        level = lane_take(whole, jnp.full((8, LANES), 40, I32)) / wtotal[...]
+            wtotal[...] = 1.0 / (lane_take(whole, jnp.full((8, LANES), 48, I32)) + 1.0)
+        level = lane_take(whole, jnp.full((8, LANES), 40, I32)) * wtotal[...]
         level = jnp.concatenate([level] * 4, 0)
         before = beta
 
-    chunks = 4
+    chunks = 2
     for b in range(rows // span):
         pieces = []
         for o in range(b * span // 16, (b + 1) * span // 16):
@@ -711,7 +717,7 @@
             update_group(g, before, level, SWEEPS - 1)
             return 0
 
-        lax.fori_loop(c * size // 32, (c + 1) * size // 32, final, 0, unroll=4)
+        lax.fori_loop(c * size // 32, (c + 1) * size // 32, final, 0, unroll=8)
         for t in range(tiles):
             copy = pltpu.make_async_copy(
                 mm.at[t, pl.ds(8 + c * size, size), :],

time: 72.1 us -> 72 us (level)
  no operation moved by 1% of the time
where the time goes in v6:
time: 72 us; the launch traced here: 71.9 us
  Pallas kernels  69 us (96%)
  local copies, waits for them, and re-layouts  2.26 us (3%)
    pallas_call x1, Pallas kernels, on_device(): pl.pallas_call(functools.partial(kernel, zsize, dims), out_shape=(jax.Sha...  69 us
    unnamed x4, local copies, waits for them, and re-layouts  2.26 us

profile of v6, /device:TPU:1, one launch (start us, length us, event | category | flops | bytes accessed | tf_op | source)
XLA Modules:
  0.0 71.9 jit_solution(14020983609540254188)
XLA Ops:
  0.6 0.0 copy-start
  0.6 0.6 copy-done
  1.3 69.0 %shard_map.68 = (f32[512,512]{1,0:T(8,128)S(1)}, f32[40,512]{1,0:T(8,128)S(1)}) custom-call(f32[512,512]{1,0:T(8,128)} %heights.1, f32[512,512]{1,0:T(8,128)} %confidence.1, s32[512,512]{1,0:T(8,128)} %survey_ids.1, s32[512,512]{1,0:T(8,128)} %seam_mask.1, f32[1,40]{1,0:T(1,128)S(1)} %bitcast.1), custom_call_target="tpu_custom_call" | custom-call | tf_op jit(solution)/shard_map/pallas_call | solution.py:820
  70.3 1.0 %copy.9 = f32[512,512]{1,0:T(8,128)} copy(f32[512,512]{1,0:T(8,128)S(1)} %get-tuple-element.4) | data formatting | bytes 2097152
  71.2 0.6 copy.10
Async XLA Ops:
  0.6 0.7 copy-start
